TPU v7x, 128 devices: a whole 4x4x4 slice. The times are simulated.
128 devices in a mesh: ctx: 16 (over z, y), head: 8 (over x, core).
Axes of the slice: x: 4, y: 4, z: 4, core: 2. Of those that a mesh axis runs over, the one named last changes fastest.
Arguments:
- tokens: bfloat16 [4096, 5120], P('ctx', 'head'), may hold values from -6 to 6
- gain: float32 [5120], P('head'), may hold values from 0.1 to 1.9
- qkv_weight: bfloat16 [5120, 7168], P('head')
- target: bfloat16 [4096, 5120], P('ctx', 'head'), may hold values from -6 to 6
- advantage: int32 [4096], P('ctx'), may hold values from -4 to 4
- segment: int32 [4096], P('ctx'), may hold values from 0 to 7, never falling along the last dimension, each value on 1 to 2048 neighbouring positions
Outputs:
- attn: bfloat16 [4096, 5120], P('ctx', 'head')
- grad_tokens: bfloat16 [4096, 5120], P('ctx', 'head')
- grad_gain: float32 [5120], P('head')
Inputs may be any that keep to these rules, and one draw needn't show every extreme that they name: segment ids never fall along the tokens; each of the 8 rollouts has 1 to 2048 tokens, one exactly 2048.
All inputs are finite; a program needn't handle non-finite values.
Results may differ from a plain program's by a relative error of at most 0.015.
Values may be sent and summed in bfloat16 or wider, within the bound.
A program may use at most 128 MiB of HBM per device.

v0:
```python
import jax
import jax.numpy as jnp
from jax import lax
from jax.sharding import PartitionSpec as P

D = 5120
QH = 40
KVH = 8
HD = 128


epsilon = 1e-06


def on_device(tokens, gain, qkv_weight, target, advantage, segment):
    local_rows = tokens.shape[0]
    features = tokens.astype(jnp.float32)
    squares = lax.psum(jnp.sum(features * features, -1), "head")
    recip = lax.rsqrt(squares[:, None] / D + epsilon)
    normed = (features * recip * gain).astype(jnp.bfloat16)
    group_cols = qkv_weight.shape[1] // lax.axis_size("head")
    groups_here = KVH // lax.axis_size("head")
    per_group = QH // KVH
    pieces = local_rows * lax.axis_size("head") // local_rows
    columns = qkv_weight
    product = jnp.dot(normed, columns, preferred_element_type=jnp.float32)
    projected = lax.psum_scatter(
        product.reshape(local_rows, pieces, group_cols)
        .transpose(1, 0, 2)
        .reshape(local_rows * lax.axis_size("head"), group_cols),
        "head",
        scatter_dimension=0,
        tiled=True,
    )
    projected = projected.astype(jnp.bfloat16).reshape(local_rows, groups_here, per_group + 2, HD)
    queries = projected[:, :, :per_group]
    pairs = projected[:, :, per_group:]
    all_pairs = lax.all_gather(pairs, "ctx", axis=0, tiled=True)
    key_segment = lax.all_gather(segment, "ctx", axis=0, tiled=True)
    key_count = all_pairs.shape[0]
    query_pos = lax.axis_index("ctx") * local_rows + jnp.arange(local_rows, dtype=jnp.int32)
    key_block = min(512, key_count)
    block_count = key_count // key_block
    scale = HD ** (-0.5)

    def scores_for(begin_row, size):
        block_pairs = lax.dynamic_slice_in_dim(all_pairs, begin_row, size, 0)
        block_seg = lax.dynamic_slice_in_dim(key_segment, begin_row, size, 0)
        key_pos = begin_row + jnp.arange(size, dtype=jnp.int32)
        visible = (segment[:, None] == block_seg[None, :]) & (
            key_pos[None, :] <= query_pos[:, None]
        )
        scores = (
            jnp.einsum(
                "tgrd,sgd->tgrs", queries, block_pairs[:, :, 0], preferred_element_type=jnp.float32
            )
            * scale
        )
        return (block_pairs, visible[:, None, None, :], scores)

    def stats_step(carry, step_index):
        begin_row = step_index * key_block
        running_max, running_sum = carry
        block_pairs, visible, scores = scores_for(begin_row, key_block)
        new_max = jnp.maximum(running_max, jnp.max(jnp.where(visible, scores, -1e30), -1))
        added = jnp.sum(jnp.where(visible, jnp.exp(scores - new_max[..., None]), 0.0), -1)
        return ((new_max, running_sum * jnp.exp(running_max - new_max) + added), None)

    stat_shape = (local_rows, groups_here, per_group)
    start_stats = (jnp.full(stat_shape, -1e30, jnp.float32), jnp.zeros(stat_shape, jnp.float32))
    (running_max, running_sum), _ = lax.scan(
        stats_step, start_stats, jnp.arange(block_count, dtype=jnp.int32)
    )
    lse = running_max + jnp.log(running_sum)

    def probs_for(visible, scores):
        return jnp.where(visible, jnp.exp(scores - lse[..., None]), 0.0)

    def output_step(accum, step_index):
        begin_row = step_index * key_block
        block_pairs, visible, scores = scores_for(begin_row, key_block)
        probs_b = probs_for(visible, scores).astype(jnp.bfloat16)
        return (
            accum
            + jnp.einsum(
                "tgrs,sgd->tgrd", probs_b, block_pairs[:, :, 1], preferred_element_type=jnp.float32
            ),
            None,
        )

    empty_out = jnp.zeros((local_rows, groups_here, per_group, HD), jnp.float32)
    output, _ = lax.scan(output_step, empty_out, jnp.arange(block_count, dtype=jnp.int32))
    attn_b = output.astype(jnp.bfloat16)
    gradout = (0.25 * advantage.astype(jnp.float32)[:, None] * target.astype(jnp.float32)).astype(
        jnp.bfloat16
    )
    gradout = gradout.reshape(local_rows, groups_here, per_group, HD)
    delta = jnp.sum(gradout.astype(jnp.float32) * attn_b.astype(jnp.float32), -1)

    def backward_step(dquery_acc, step_index):
        begin_row = step_index * key_block
        block_pairs, visible, scores = scores_for(begin_row, key_block)
        probs = probs_for(visible, scores)
        dprobs = jnp.einsum(
            "tgrd,sgd->tgrs", gradout, block_pairs[:, :, 1], preferred_element_type=jnp.float32
        )
        dscores = (probs * (dprobs - delta[..., None]) * scale).astype(jnp.bfloat16)
        new_dquery = dquery_acc + jnp.einsum(
            "tgrs,sgd->tgrd", dscores, block_pairs[:, :, 0], preferred_element_type=jnp.float32
        )
        dkey = jnp.einsum("tgrs,tgrd->sgd", dscores, queries, preferred_element_type=jnp.float32)
        dvalue = jnp.einsum(
            "tgrs,tgrd->sgd",
            probs.astype(jnp.bfloat16),
            gradout,
            preferred_element_type=jnp.float32,
        )
        return (new_dquery, jnp.stack([dkey, dvalue], 2))

    dquery, block_grads = lax.scan(
        backward_step, empty_out, jnp.arange(block_count, dtype=jnp.int32)
    )
    pair_grads = block_grads.reshape(key_count, groups_here, 2, HD)
    key_grads = lax.psum_scatter(
        pair_grads.astype(jnp.bfloat16), "ctx", scatter_dimension=0, tiled=True
    )
    dproj = jnp.concatenate([dquery.astype(jnp.bfloat16), key_grads], axis=2)
    dproj = dproj.reshape(local_rows, group_cols)
    columns = qkv_weight
    dnormed = lax.dot_general(
        lax.all_gather(dproj, "head", axis=1, tiled=True),
        columns,
        (((1,), (1,)), ((), ())),
        preferred_element_type=jnp.float32,
    )
    grad_gain = lax.psum(jnp.sum(dnormed * features * recip, 0), "ctx")
    scaled = dnormed * gain
    inner = lax.psum(jnp.sum(scaled * features, -1), "head")
    grad_tokens = (recip * scaled - features * recip**3 * inner[:, None] / D).astype(jnp.bfloat16)
    return (attn_b.reshape(local_rows, groups_here * per_group * HD), grad_tokens, grad_gain)


def solution(mesh):
    placed = (P("ctx", "head"), P("head"), P("head", None), P("ctx", "head"), P("ctx"), P("ctx"))
    return jax.shard_map(
        on_device,
        mesh=mesh,
        in_specs=placed,
        out_specs=(P("ctx", "head"), P("ctx", "head"), P("head")),
        check_vma=False,
    )
```

profile of v0, /device:TPU:0, one launch (start us, length us, event | category | flops | bytes accessed | tf_op | source)
XLA Modules:
  0.0 459.5 jit_solution(2480041039995572210)
XLA Ops:
  8.3 14.7 %psum.21 = f32[256]{0:T(256)S(1)} all-reduce(f32[256]{0:T(256)S(1)} %fusion.53), channel_id=1, replica_groups=mesh['ctx'=16,'head'=8] {'head'}, use_global_device_ids=true, to_apply=%region_1.0 | all-reduce | flops 256 | bytes 2048 | tf_op jit(solution)/shard_map/psum | solution.py:18
  23.0 5.7 %fusion.63 = f32[256,7168]{1,0:T(8,128)S(1)} fusion(bf16[640,7168]{1,0:T(8,128)(2,1)} %param.14, bf16[256,640]{1,0:T(8,128)(2,1)} %param.12, f32[640]{0:T(1024)} %param.13, f32[256]{0:T(256)S(1)} %get-tuple-element.407), kind=kOutput, calls=%fused_computation.92 | convolution fusion | flops 2349465600 | bytes 16846336 | tf_op jit(solution)/shard_map/dot_general | solution.py:26
  28.7 3.5 copy.63
  32.3 47.4 %reduce-scatter.3.cloned.1.call-done = f32[256,896]{1,0:T(8,128)} async-done(((f32[2048,896]{1,0:T(8,128)}), f32[256,896]{1,0:T(8,128)}) %reduce-scatter.3.cloned.1.call-update) | async-done | bytes 917520 | tf_op jit(solution)/shard_map/reduce_scatter | solution.py:27
  83.1 23.5 %all-gather = s32[16,1,256]{2,1,0:T(1,128)S(1)} all-gather(s32[1,1,256]{2,1,0:T(1,128)S(1)} %bitcast.307), channel_id=1, replica_groups=mesh['ctx'=16,'head'=8] {'ctx'}, dimensions={0}, use_global_device_ids=true | all-gather | bytes 17408 | tf_op jit(solution)/shard_map/all_gather | solution.py:39
  106.9 23.0 %all-gather.4.cloned.1.call-done = bf16[4096,1,2,128]{0,3,2,1:T(8,128)(2,1)} async-done(((bf16[256,1,2,128]{0,3,2,1:T(8,128)(2,1)}), bf16[4096,1,2,128]{0,3,2,1:T(8,128)(2,1)}) %all-gather.4.cloned.1.call-update) | async-done | bytes 2097168 | tf_op jit(solution)/shard_map/all_gather | solution.py:38
  129.9 4.1 copy.40
  134.0 29.2 %while.37 = (s32[]{:T(128)}, f32[256,1,5]{0,2,1:T(8,128)S(1)}, f32[256,1,5]{0,2,1:T(8,128)S(1)}, s32[256]{0:T(256)S(1)}, s32[8]{0:T(128)S(1)}, /*index=5*/s32[40...) while((s32[]{:T(128)}, f32[256,1,5]{0,2,1:T(8,128)S(1)}, ...), condition=%wide.region_6.7_spmd.clone, body=%wide.region_3.6_spmd.clone.sunk | while | flops 172760064 | bytes 6174930 | solution.py:71
  135.5 1.5 fusion.88
  139.2 1.5 fusion.88
  142.8 1.5 fusion.88
  146.5 1.5 fusion.88
  150.1 1.5 fusion.88
  153.8 1.5 fusion.88
  157.4 1.5 fusion.88
  161.1 1.5 fusion.88
  163.3 35.2 %while.38 = (s32[]{:T(128)}, f32[256,1,5,128]{0,3,2,1:T(8,128)}, s32[8]{0:T(128)S(1)}, bf16[4096,1,2,128]{3,0,2,1:T(8,128)(2,1)}, s32[256]{0:T(256)S(1)}, /*inde...) while((s32[]{:T(128)}, f32[256,1,5,128]{0,3,2,1:T(8,128)}, ...), condition=%wide.region_8.9_spmd.clone, body=%wide.region_7.8_spmd.clone.sunk | while | flops 338887424 | bytes 2183392 | solution.py:92
  164.8 2.6 fusion.91
  169.0 2.9 fusion.91
  173.4 2.9 fusion.91
  177.9 2.9 fusion.91
  182.3 2.9 fusion.91
  186.7 2.9 fusion.91
  191.2 2.9 fusion.91
  195.6 2.9 fusion.91
  199.7 85.1 %while.39 = (s32[]{:T(128)}, f32[256,1,5,128]{0,3,2,1:T(8,128)S(1)}, bf16[8,512,1,2,128]{4,1,0,3,2:T(8,128)(2,1)}, s32[8]{0:T(128)S(1)}, bf16[4096,1,2,128]{3,0,...) while((s32[]{:T(128)}, ...), condition=%wide.region_11.12_spmd.clone, body=%wide.region_10.11_spmd.clone.sunk | while | flops 847315712 | bytes 26506020 | solution.py:120
  201.2 2.9 fusion.99
  204.2 2.9 fusion.100
  211.9 2.9 fusion.99
  214.8 2.9 fusion.100
  222.5 2.9 fusion.99
  225.4 2.9 fusion.100
  233.1 2.9 fusion.99
  236.1 2.9 fusion.100
  240.9 1.4 fusion.101
  243.8 2.9 fusion.99
  246.7 2.9 fusion.100
  254.4 2.9 fusion.99
  257.3 2.9 fusion.100
  265.1 2.9 fusion.99
  268.0 2.9 fusion.100
  275.7 2.9 fusion.99
  278.6 2.9 fusion.100
  285.1 73.6 %reduce-scatter.5.cloned.1.call-done = bf16[256,1,2,128]{3,0,2,1:T(8,128)(2,1)} async-done(((bf16[4096,1,2,128]{3,0,2,1:T(8,128)(2,1)}), bf16[256,1,2,128]{3,0,2,1:T(8,128)(2,1)}) %reduce-scatter.5.cloned.1.call-update) | async-done | bytes 131088 | tf_op jit(solution)/shard_map/reduce_scatter | solution.py:124
  361.5 28.3 %all-gather.6.cloned.1.call-done = bf16[256,7168]{0,1:T(8,128)(2,1)} async-done(((bf16[256,896]{0,1:T(8,128)(2,1)}), bf16[256,7168]{0,1:T(8,128)(2,1)}) %all-gather.6.cloned.1.call-update) | async-done | bytes 3670032 | tf_op jit(solution)/shard_map/all_gather | solution.py:131
  389.8 7.9 %fusion.62 = (f32[640]{0:T(1024)S(1)}, f32[256]{0:T(256)S(1)}, f32[256,640]{1,0:T(8,128)S(1)}) fusion(bf16[256,640]{1,0:T(8,128)(2,1)S(1)} %copy-done.2, f32[256]{0:T(256)S(1)} %get-tuple-element.407, f32[640]{0:T(1024)S(1)} %copy-done.6, bf16[256,7168]{0,1:T(8,128)(2,1)} %all-gather.6.cloned.1.call-done, bf16[640,7168]{1,0:T(8,128)(2,1)} %param.14), kind=kOutput, calls=%fused_computation.88 | convolution fusion | flops 2349956352 | bytes 13835264 | tf_op jit(solution)/shard_map/dot_general | solution.py:130
  397.7 13.2 %psum.22 = f32[256]{0:T(256)S(1)} all-reduce(f32[256]{0:T(256)S(1)} %get-tuple-element.341), channel_id=1, replica_groups=mesh['ctx'=16,'head'=8] {'head'}, use_global_device_ids=true, to_apply=%region_14.15 | all-reduce | flops 256 | bytes 2048 | tf_op jit(solution)/shard_map/psum | solution.py:138
  410.9 41.1 %psum.23 = f32[640]{0:T(1024)} all-reduce(f32[640]{0:T(1024)S(1)} %get-tuple-element.340), channel_id=1, replica_groups=mesh['ctx'=16,'head'=8] {'ctx'}, use_global_device_ids=true, to_apply=%region_16.17 | all-reduce | flops 640 | bytes 5120 | tf_op jit(solution)/shard_map/psum | solution.py:136
  (247 shorter events, 59.9 us)
Async XLA Ops:
  7.2 72.5 %reduce-scatter.3.cloned.1.call-start = ((), (), s32[]{:S(2)}) async-start(), calls=%async_computation.2 | async-start | bytes 8257536 | tf_op jit(solution)/shard_map/reduce_scatter | solution.py:27
  32.2 49.7 %copy-start.3 = (bf16[256,640]{1,0:T(8,128)(2,1)S(1)}, bf16[256,640]{1,0:T(8,128)(2,1)}, u32[]{:S(2)}) copy-start(bf16[256,640]{1,0:T(8,128)(2,1)} %param.15) | copy-start | bytes 983044
  32.2 49.9 %copy-start.7 = (s32[256]{0:T(256)S(1)}, s32[256]{0:T(256)}, u32[]{:S(2)}) copy-start(s32[256]{0:T(256)} %param.16) | copy-start | bytes 3076
  32.2 50.9 %copy-start.5 = (s32[256]{0:T(256)S(1)}, s32[256]{0:T(256)}, u32[]{:S(2)}) copy-start(s32[256]{0:T(256)} %param.17) | copy-start | bytes 3076
  32.2 97.6 %all-gather.4.cloned.1.call-start = ((), (), s32[]{:S(2)}) async-start(), calls=%async_computation.3 | async-start | bytes 2228224 | tf_op jit(solution)/shard_map/all_gather | solution.py:38
  81.8 276.9 %reduce-scatter.5.cloned.1.call-start = ((), (), s32[]{:S(2)}) async-start(), calls=%async_computation.4 | async-start | bytes 2228224 | tf_op jit(solution)/shard_map/reduce_scatter | solution.py:124
  163.2 36.4 %copy-start.1 = (f32[256,1,5,128]{0,3,2,1:T(8,128)S(1)}, f32[256,1,5,128]{0,3,2,1:T(8,128)}, u32[]{:S(2)}) copy-start(f32[256,1,5,128]{0,3,2,1:T(8,128)} %custom-call.3) | copy-start | bytes 1966084
  163.2 36.4 %copy-start.4 = (bf16[256,1,5,128]{3,0,2,1:T(8,128)(2,1)S(1)}, bf16[256,1,5,128]{3,0,2,1:T(8,128)(2,1)}, u32[]{:S(2)}) copy-start(bf16[256,1,5,128]{3,0,2,1:T(8,128)(2,1)} %copy.45) | copy-start | bytes 983044
  204.2 3.4 copy-start
  214.8 3.4 copy-start
  225.4 3.4 copy-start
  236.1 3.4 copy-start
  246.7 3.4 copy-start
  257.3 3.4 copy-start
  268.0 3.4 copy-start
  278.6 3.4 copy-start
  284.8 105.0 %copy-start.2 = (bf16[256,640]{1,0:T(8,128)(2,1)S(1)}, bf16[256,640]{1,0:T(8,128)(2,1)}, u32[]{:S(2)}) copy-start(bf16[256,640]{1,0:T(8,128)(2,1)} %param.12) | copy-start | bytes 983044
  284.8 105.0 %copy-start.6 = (f32[640]{0:T(1024)S(1)}, f32[640]{0:T(1024)}, u32[]{:S(2)}) copy-start(f32[640]{0:T(1024)} %param.13) | copy-start | bytes 7684
  284.8 104.9 %all-gather.6.cloned.1.call-start = ((), (), s32[]{:S(2)}) async-start(), calls=%async_computation.5 | async-start | bytes 4128768 | tf_op jit(solution)/shard_map/all_gather | solution.py:131
Sparse Core Ops, SparseCore 0:
  32.3 47.3 reduce-scatter.2
  82.4 47.4 all-gather.3
  285.0 73.7 reduce-scatter.4
  360.7 29.0 all-gather.5
where the time goes:
time: 461 us; the launch traced here: 460 us
  waiting for transfers between devices  172 us (37%)
  matrix products  115 us (25%)
  blocking collectives  92.6 us (20%)
  local copies, waits for them, and re-layouts  27.7 us (6%)
  other arithmetic  20.9 us (5%)
  loops' own time  16.9 us (4%)
  between operations  14 us (3%)
    reduce_scatter x1, waiting for transfers between devices, on_device(): lax.psum_scatter(pair_grads.astype(jnp.bfloat16), 'ctx', scatter_dimensio...  73.6 us
    reduce_scatter x1, waiting for transfers between devices, on_device(): lax.psum_scatter(product.reshape(local_rows, pieces, group_cols).transpos...  47.4 us
    psum x1, blocking collectives, on_device(): grad_gain = lax.psum(jnp.sum(dnormed * features * recip, 0), 'ctx')  41.1 us
    dot_general x16, matrix products, scores_for(): jnp.einsum('tgrd,sgd->tgrs', queries, block_pairs[:, :, 0], preferred_ele...  35.2 us
    all_gather x1, waiting for transfers between devices, on_device(): lax.all_gather(dproj, 'head', axis=1, tiled=True)  28.3 us
    all_gather x1, blocking collectives, on_device(): key_segment = lax.all_gather(segment, 'ctx', axis=0, tiled=True)  23.5 us
    dot_general x8, matrix products, backward_step(): jnp.einsum('tgrd,sgd->tgrs', gradout, block_pairs[:, :, 1], preferred_ele...  23.3 us
    all_gather x1, waiting for transfers between devices, on_device(): all_pairs = lax.all_gather(pairs, 'ctx', axis=0, tiled=True)  23 us
  transfers between devices with their start and end apart: 4, of which 4 were waited for; matrix products, arithmetic and copies ran while one was open for 1% of the time, Pallas kernels for 0%

commit v1 on v0

v1 whole, which is shorter than its diff:
```python
import functools

import jax
import jax.numpy as jnp
from jax import lax
from jax.experimental import pallas as pl
from jax.experimental.pallas import tpu as pltpu
from jax.sharding import PartitionSpec as P

D = 5120
HD = 128
HEADS = 5
WINDOW = 8
EPSILON = 1e-06
SCALE = HD**-0.5
LOG2E = 1.4426950408889634
EXP_SCALE = SCALE * LOG2E
HIDDEN = -1e30
PIECES = ((640, 256), (0, 256), (256, 256), (512, 128))
STEPS = (2, 1, 3, 0)
F32 = jnp.float32
BF16 = jnp.bfloat16


def kernel(
    n_ctx, tok, gain, w_hbm, target, advantage, segment,
    attn, grad_tokens, grad_gain,
    xb, wv, part_send, part_recv, chip_sum, hold, own, relay, landed,
    stats, recip, seg_win, key_win, value_win, key_t, value_t, bias,
    q_rows, q_t, go_t, scores, expo, out_t, gp_rows, gp_t, dq_t, pair_acc, pair_send, pair_recv,
    dproj, inner_stats, dnormed, gain_stats,
    w_sem, ps_send, ps_recv, r1_send, r1_recv, r2_send, r2_recv, st_send, st_recv,
    seg_send, seg_recv, k_send, k_recv, v_send, v_recv, pair_ssem, pair_rsem,
    ag_send, ag_recv, in_send, in_recv, gg_send, gg_recv,
):
    rows = tok.shape[0]
    half = rows // 2
    c = lax.axis_index("ctx")
    h = lax.axis_index("head")
    x = h // 2
    p = lax.rem(h, 2)

    def head_of(xx, pp):
        return lax.rem(xx + 8, 4) * 2 + pp

    right, left, partner = head_of(x + 1, p), head_of(x - 1, p), head_of(x, 1 - p)
    started = []

    def remote(src, dst, send, recv, **where):
        axis, index = next(iter(where.items()))
        return pltpu.make_async_remote_copy(
            src_ref=src, dst_ref=dst, send_sem=send, recv_sem=recv,
            device_id={axis: index}, device_id_type=pl.DeviceIdType.MESH,
        )

    def start(copy, when=None):
        started.append((copy, when))
        if when is None:
            copy.start()
        else:
            pl.when(when)(copy.start)

    def arrived(dst, recv):
        remote(dst, dst, recv, recv, head=partner).wait_recv()

    barrier = pltpu.get_barrier_semaphore()
    for d in range(1, 8):
        pl.semaphore_signal(
            barrier, inc=1, device_id={"head": lax.rem(h + d, 8)}, device_id_type=pl.DeviceIdType.MESH
        )
    for d in range(1, n_ctx):
        pl.semaphore_signal(
            barrier, inc=1, device_id={"ctx": lax.rem(c + d, n_ctx)}, device_id_type=pl.DeviceIdType.MESH
        )

    def fetch(s, i):
        off, wide = PIECES[s]
        g = head_of(x + STEPS[i % 4], (1 - p) if i < 4 else p)
        first = pl.multiple_of(g * 896 + off, 128)
        return g, pltpu.make_async_copy(
            w_hbm.at[:, pl.ds(first, wide)], wv.at[g, :, pl.ds(off, wide)], w_sem.at[s, i]
        )

    for s in range(4):
        for i in range(8):
            fetch(s, i)[1].start()

    features = tok[...].astype(F32)
    xb[...] = (features * gain[...]).astype(BF16)
    stats[h] = lax.dot_general(
        jnp.ones((8, tok.shape[1]), F32), features * features, (((1,), (1,)), ((), ())),
        precision=lax.Precision.HIGHEST, preferred_element_type=F32,
    )
    seg_win[0] = jnp.broadcast_to(segment[...].astype(F32), (16, rows)).astype(BF16)

    pl.semaphore_wait(barrier, 7 + n_ctx - 1)

    def project(s):
        off, wide = PIECES[s]
        cols = pl.ds(off, wide)
        for i in range(4):
            g, copy = fetch(s, i)
            copy.wait()
            part_send[i, :, off : off + wide] = jnp.dot(
                xb[...], wv[g, :, off : off + wide], preferred_element_type=F32
            ).astype(BF16)
            start(remote(
                part_send.at[i, :, cols], part_recv.at[i, :, cols],
                ps_send.at[s, i], ps_recv.at[s, i], head=partner,
            ))
        for i in range(4):
            g, copy = fetch(s, 4 + i)
            copy.wait()
            mine = jnp.dot(xb[...], wv[g, :, off : off + wide], preferred_element_type=F32)
            arrived(part_recv.at[i, :, cols], ps_recv.at[s, i])
            mine = mine + part_recv[i, :, off : off + wide].astype(F32)
            if i < 3:
                chip_sum[i, :, off : off + wide] = mine.astype(BF16)
            top = pl.ds(0, half)
            low = pl.ds(half, half)
            if i == 0:
                start(remote(
                    chip_sum.at[0, top, cols], relay.at[0, :, cols],
                    r1_send.at[s, 0], r1_recv.at[s, 0], head=right,
                ))
                start(remote(
                    chip_sum.at[0, low, cols], relay.at[1, :, cols],
                    r1_send.at[s, 1], r1_recv.at[s, 1], head=left,
                ))
            elif i == 1:
                hold[0, :, off : off + wide] = mine[:half]
                start(remote(
                    chip_sum.at[1, low, cols], landed.at[0, low, cols],
                    r2_send.at[s, 0], r2_recv.at[s, 0], head=right,
                ))
            elif i == 2:
                hold[1, :, off : off + wide] = mine[half:]
                start(remote(
                    chip_sum.at[2, top, cols], landed.at[1, top, cols],
                    r2_send.at[s, 1], r2_recv.at[s, 1], head=left,
                ))
            else:
                own[:, off : off + wide] = mine

    def pass_on(s):
        off, wide = PIECES[s]
        cols = pl.ds(off, wide)
        top = pl.ds(0, half)
        low = pl.ds(half, half)
        arrived(relay.at[0, :, cols], r1_recv.at[s, 0])
        chip_sum[1, :half, off : off + wide] = (
            hold[0, :, off : off + wide] + relay[0, :, off : off + wide].astype(F32)
        ).astype(BF16)
        start(remote(
            chip_sum.at[1, top, cols], landed.at[0, top, cols],
            r2_send.at[s, 2], r2_recv.at[s, 2], head=right,
        ))
        arrived(relay.at[1, :, cols], r1_recv.at[s, 1])
        chip_sum[2, half:, off : off + wide] = (
            hold[1, :, off : off + wide] + relay[1, :, off : off + wide].astype(F32)
        ).astype(BF16)
        start(remote(
            chip_sum.at[2, low, cols], landed.at[1, low, cols],
            r2_send.at[s, 3], r2_recv.at[s, 3], head=left,
        ))

    def finish(s):
        off, wide = PIECES[s]
        cols = pl.ds(off, wide)
        top = pl.ds(0, half)
        low = pl.ds(half, half)
        arrived(landed.at[0, low, cols], r2_recv.at[s, 0])
        arrived(landed.at[1, top, cols], r2_recv.at[s, 1])
        arrived(landed.at[0, top, cols], r2_recv.at[s, 2])
        arrived(landed.at[1, low, cols], r2_recv.at[s, 3])
        total = own[:, off : off + wide] + landed[0, :, off : off + wide].astype(F32)
        total = total + landed[1, :, off : off + wide].astype(F32)
        scale = recip[:, :1]
        return (total * scale).astype(BF16)

    project(0)
    for d in range(1, 8):
        start(remote(
            stats.at[h], stats.at[h], st_send.at[d], st_recv.at[h], head=lax.rem(h + d, 8),
        ))
    for j in range(1, WINDOW + 1):
        start(remote(
            seg_win.at[0], seg_win.at[j], seg_send.at[j], seg_recv.at[j],
            ctx=jnp.minimum(c + j, n_ctx - 1),
        ), c + j < n_ctx)
    pass_on(0)
    project(1)
    for d in range(1, 8):
        sender = lax.rem(h + d, 8)
        arrived(stats.at[sender], st_recv.at[sender])
    squares = jnp.sum(stats[...], 0)
    recip[...] = jnp.broadcast_to(
        lax.rsqrt(jnp.transpose(squares)[:, :1] / D + EPSILON), (rows, HD)
    )

    pair = finish(0)
    key_win[0] = pair[:, :HD]
    value_win[0] = pair[:, HD:]
    for j in range(1, WINDOW + 1):
        later = jnp.minimum(c + j, n_ctx - 1)
        start(remote(key_win.at[0], key_win.at[j], k_send.at[j], k_recv.at[j], ctx=later), c + j < n_ctx)
        start(remote(value_win.at[0], value_win.at[j], v_send.at[j], v_recv.at[j], ctx=later), c + j < n_ctx)

    pass_on(1)
    project(2)
    pass_on(2)
    project(3)
    pass_on(3)

    factor = 0.25 * advantage[...].astype(F32)
    for r in range(HEADS):
        block = jnp.transpose(target[:, r * HD : (r + 1) * HD].astype(F32))
        go_t[:, r * rows : (r + 1) * rows] = (block * factor).astype(BF16)

    def queries(s):
        q = finish(s)
        first = PIECES[s][0] // HD
        for i in range(PIECES[s][1] // HD):
            one = q[:, i * HD : (i + 1) * HD]
            q_rows[(first + i) * rows : (first + i + 1) * rows] = one
            q_t[:, (first + i) * rows : (first + i + 1) * rows] = jnp.transpose(one.astype(F32)).astype(BF16)

    queries(1)

    blocks = jnp.minimum(c, WINDOW) + 1
    q_seg = seg_win[0, :1].astype(F32)

    def prepare(j, diagonal):
        key_t[j] = jnp.transpose(key_win[j].astype(F32)).astype(BF16)
        value_t[j] = jnp.transpose(value_win[j].astype(F32)).astype(BF16)
        k_seg = jnp.transpose(seg_win[j].astype(F32))[:, :1]
        visible = k_seg == q_seg
        if diagonal:
            k_pos = lax.broadcasted_iota(jnp.int32, (rows, rows), 0)
            q_pos = lax.broadcasted_iota(jnp.int32, (rows, rows), 1)
            visible = visible & (k_pos <= q_pos)
        bias[j] = jnp.where(visible, 0.0, HIDDEN)

    prepare(0, True)

    @pl.loop(1, blocks)
    def _(j):
        arrived(seg_win.at[j], seg_recv.at[j])
        arrived(key_win.at[j], k_recv.at[j])
        arrived(value_win.at[j], v_recv.at[j])
        prepare(j, False)

    def attend(s, fresh):
        off, wide = PIECES[s]
        heads = wide // HD
        n = heads * rows
        first = off // HD * rows
        span = slice(first, first + n)

        def score_block(j, top):
            block = jnp.dot(key_win[j], q_t[:, span], preferred_element_type=F32)
            block = block + jnp.concatenate([bias[j]] * heads, axis=1)
            scores[j, :, :n] = block
            return jnp.maximum(top, jnp.max(block.reshape(rows // 8, 8, n), 0))

        top = lax.fori_loop(0, blocks, score_block, jnp.full((8, n), HIDDEN, F32))
        top = jnp.max(top, 0, keepdims=True) * EXP_SCALE
        out_t[:, :n] = jnp.zeros((HD, n), F32)

        def expo_block(j, total):
            e = jnp.exp2(scores[j, :, :n] * EXP_SCALE - top)
            eb = e.astype(BF16)
            expo[j, :, :n] = eb
            out_t[:, :n] += jnp.dot(value_t[j], eb, preferred_element_type=F32)
            return total + jnp.sum(e.reshape(rows // 8, 8, n), 0)

        total = lax.fori_loop(0, blocks, expo_block, jnp.zeros((8, n), F32))
        inverse = 1.0 / jnp.sum(total, 0, keepdims=True)
        out_b = (out_t[:, :n] * inverse).astype(BF16).astype(F32)
        go = go_t[:, span].astype(F32)
        delta = jnp.sum(go * out_b, 0, keepdims=True) * inverse
        scaled = go * inverse
        gp_t[:, :n] = scaled.astype(BF16)
        for i in range(heads):
            r = off // HD + i
            attn[:, r * HD : (r + 1) * HD] = jnp.transpose(out_b[:, i * rows : (i + 1) * rows]).astype(BF16)
            gp_rows[i * rows : (i + 1) * rows] = jnp.transpose(scaled[:, i * rows : (i + 1) * rows]).astype(BF16)
        dq_t[:, :n] = jnp.zeros((HD, n), F32)

        @pl.loop(0, blocks)
        def _(j):
            dp = jnp.dot(value_win[j], gp_t[:, :n], preferred_element_type=F32)
            eb = expo[j, :, :n]
            ds = (eb.astype(F32) * (dp - delta)).astype(BF16)
            dk = jnp.dot(ds, q_rows[span], preferred_element_type=F32)
            dv = jnp.dot(eb, gp_rows[:n], preferred_element_type=F32)
            if fresh:
                pair_acc[j, :, :HD] = dk
                pair_acc[j, :, HD:] = dv
            else:
                pair_acc[j, :, :HD] += dk
                pair_acc[j, :, HD:] += dv
            dq_t[:, :n] += jnp.dot(key_t[j], ds, preferred_element_type=F32)

        inner = jnp.zeros((1, rows), F32)
        for i in range(heads):
            r = off // HD + i
            one = dq_t[:, i * rows : (i + 1) * rows] * SCALE
            dproj[h, :, r * HD : (r + 1) * HD] = jnp.transpose(one).astype(BF16)
            inner += jnp.sum(one * q_t[:, r * rows : (r + 1) * rows].astype(F32), 0, keepdims=True)
        return inner

    def slot(ref, s, who, lo, size):
        off, wide = PIECES[s]
        return ref.at[who, pl.ds(lo, size), pl.ds(off, wide)]

    def move(s, n, who, lo, size, to):
        start(remote(slot(dproj, s, who, lo, size), slot(dproj, s, who, lo, size),
                     ag_send.at[s, n], ag_recv.at[s, n], head=to))

    def landed_piece(s, n, who, lo, size):
        arrived(slot(dproj, s, who, lo, size), ag_recv.at[s, n])

    far = head_of(x + 2, p)

    def gather_send(s):
        move(s, 0, h, 0, rows, right)
        move(s, 1, h, 0, rows, left)
        move(s, 2, h, 0, rows, partner)

    def gather_pass(s):
        landed_piece(s, 0, left, 0, rows)
        move(s, 3, left, 0, half, right)
        move(s, 5, left, 0, rows, partner)
        landed_piece(s, 1, right, 0, rows)
        move(s, 4, right, half, half, left)
        move(s, 6, right, 0, rows, partner)

    def gather_far(s):
        landed_piece(s, 3, far, 0, half)
        move(s, 7, far, 0, half, partner)
        landed_piece(s, 4, far, half, half)
        move(s, 8, far, half, half, partner)

    def add(s, who, fresh=False):
        off, wide = PIECES[s]
        value = lax.dot_general(
            dproj[who, :, off : off + wide], wv[who, :, off : off + wide],
            (((1,), (1,)), ((), ())), preferred_element_type=F32,
        )
        if fresh:
            dnormed[...] = value
        else:
            dnormed[...] += value

    def add_own(s, fresh=False):
        add(s, h, fresh)
        add(s, left)
        add(s, right)

    def add_rest(s):
        add(s, far)
        landed_piece(s, 2, partner, 0, rows)
        add(s, partner)
        landed_piece(s, 5, head_of(x - 1, 1 - p), 0, rows)
        add(s, head_of(x - 1, 1 - p))
        landed_piece(s, 6, head_of(x + 1, 1 - p), 0, rows)
        add(s, head_of(x + 1, 1 - p))
        other = head_of(x + 2, 1 - p)
        landed_piece(s, 7, other, 0, half)
        landed_piece(s, 8, other, half, half)
        add(s, other)

    inner = attend(1, True)
    gather_send(1)
    queries(2)
    inner += attend(2, False)
    gather_pass(1)
    gather_send(2)
    queries(3)
    inner += attend(3, False)
    gather_far(1)
    gather_pass(2)
    gather_send(3)

    for j in range(WINDOW, 0, -1):
        earlier = jnp.maximum(c - j, 0)

        def send_pair(j=j):
            pair_send[j, :, :HD] = (pair_acc[j, :, :HD] * SCALE).astype(BF16)
            pair_send[j, :, HD:] = pair_acc[j, :, HD:].astype(BF16)

        pl.when(c >= j)(send_pair)
        start(remote(
            pair_send.at[j], pair_recv.at[j], pair_ssem.at[j], pair_rsem.at[j], ctx=earlier,
        ), c >= j)

    add_own(1, True)
    gather_far(2)
    gather_pass(3)
    add_rest(1)
    add_own(2)
    gather_far(3)
    add_rest(2)
    add_own(3)
    add_rest(3)

    pair_acc[0, :, :HD] = pair_acc[0, :, :HD] * SCALE

    @pl.loop(1, jnp.minimum(n_ctx - 1 - c, WINDOW) + 1)
    def _(j):
        arrived(pair_recv.at[j], pair_rsem.at[j])
        pair_acc[0] += pair_recv[j].astype(F32)

    pair_grad = pair_acc[0]
    dproj[h, :, PIECES[0][0] :] = pair_grad.astype(BF16)
    gather_send(0)
    prod = pair_grad[:, :HD] * key_win[0].astype(F32) + pair_grad[:, HD:] * value_win[0].astype(F32)
    inner += jnp.sum(jnp.transpose(prod), 0, keepdims=True)
    inner_stats[h] = jnp.broadcast_to(inner, (8, rows))
    for d in range(1, 8):
        start(remote(
            inner_stats.at[h], inner_stats.at[h], in_send.at[d], in_recv.at[h], head=lax.rem(h + d, 8),
        ))
    gather_pass(0)
    add_own(0)
    gather_far(0)
    for d in range(1, 8):
        sender = lax.rem(h + d, 8)
        arrived(inner_stats.at[sender], in_recv.at[sender])
    add_rest(0)

    scale = recip[:, :1]
    weighted = tok[...].astype(F32) * scale
    gain_part = jnp.sum(dnormed[...] * weighted, 0, keepdims=True)
    lanes = tok.shape[1] // 128
    gain_stats[c] = jnp.zeros((8, 128), F32)
    for k in range(lanes):
        gain_stats[c, k : k + 1] = gain_part[:, k * 128 : (k + 1) * 128]
    for d in range(1, n_ctx):
        start(remote(
            gain_stats.at[c], gain_stats.at[c], gg_send.at[d], gg_recv.at[c], ctx=lax.rem(c + d, n_ctx),
        ))
    inner_col = jnp.transpose(jnp.sum(inner_stats[...], 0))[:, :1]
    grad_tokens[...] = (
        dnormed[...] * gain[...] * scale - weighted * (scale * inner_col * (1.0 / D))
    ).astype(BF16)
    for d in range(1, n_ctx):
        sender = lax.rem(c + d, n_ctx)
        arrived(gain_stats.at[sender], gg_recv.at[sender])
    gain_total = jnp.sum(gain_stats[...], 0)
    for k in range(lanes):
        grad_gain[:, k * 128 : (k + 1) * 128] = gain_total[k : k + 1]

    for copy, when in started:
        if when is None:
            copy.wait_send()
        else:
            pl.when(when)(copy.wait_send)


def on_device(n_ctx, tokens, gain, qkv_weight, target, advantage, segment):
    rows, wide = tokens.shape
    group = qkv_weight.shape[1] // 8
    n = 2 * rows
    slots = WINDOW + 1
    vmem = pl.BlockSpec(memory_space=pltpu.VMEM)
    scratch = [
        ((rows, wide), BF16), ((8, wide, group), BF16),
        ((4, rows, group), BF16), ((4, rows, group), BF16), ((3, rows, group), BF16),
        ((2, rows // 2, group), F32), ((rows, group), F32),
        ((2, rows // 2, group), BF16), ((2, rows, group), BF16),
        ((8, 8, rows), F32), ((rows, HD), F32), ((slots, 16, rows), BF16),
        ((slots, rows, HD), BF16), ((slots, rows, HD), BF16),
        ((slots, HD, rows), BF16), ((slots, HD, rows), BF16), ((slots, rows, rows), F32),
        ((HEADS * rows, HD), BF16), ((HD, HEADS * rows), BF16), ((HD, HEADS * rows), BF16),
        ((slots, rows, n), F32), ((slots, rows, n), BF16), ((HD, n), F32),
        ((n, HD), BF16), ((HD, n), BF16), ((HD, n), F32),
        ((slots, rows, 2 * HD), F32), ((slots, rows, 2 * HD), BF16), ((slots, rows, 2 * HD), BF16),
        ((8, rows, group), BF16), ((8, 8, rows), F32), ((rows, wide), F32), ((n_ctx, 8, 128), F32),
    ]
    sems = [
        (4, 8), (4, 4), (4, 4), (4, 2), (4, 2), (4, 4), (4, 4), (8,), (8,),
        (slots,), (slots,), (slots,), (slots,), (slots,), (slots,), (slots,), (slots,),
        (4, 9), (4, 9), (8,), (8,), (n_ctx,), (n_ctx,),
    ]
    out, grad_tokens, grad_gain = pl.pallas_call(
        functools.partial(kernel, n_ctx),
        out_shape=(
            jax.ShapeDtypeStruct((rows, HEADS * HD), BF16),
            jax.ShapeDtypeStruct((rows, wide), BF16),
            jax.ShapeDtypeStruct((1, wide), F32),
        ),
        in_specs=[vmem, vmem, pl.BlockSpec(memory_space=pl.ANY), vmem, vmem, vmem],
        out_specs=(vmem, vmem, vmem),
        scratch_shapes=[pltpu.VMEM(shape, dtype) for shape, dtype in scratch]
        + [pltpu.SemaphoreType.DMA(shape) for shape in sems],
        compiler_params=pltpu.CompilerParams(
            collective_id=0, has_side_effects=True, vmem_limit_bytes=60 * 1024 * 1024
        ),
    )(
        tokens, gain.reshape(1, wide), qkv_weight, target,
        advantage.reshape(1, rows), segment.reshape(1, rows),
    )
    return out, grad_tokens, grad_gain.reshape(wide)


def solution(mesh):
    placed = (P("ctx", "head"), P("head"), P("head", None), P("ctx", "head"), P("ctx"), P("ctx"))
    return jax.shard_map(
        functools.partial(on_device, mesh.shape["ctx"]),
        mesh=mesh,
        in_specs=placed,
        out_specs=(P("ctx", "head"), P("ctx", "head"), P("head")),
        check_vma=False,
    )
```

time: 461 us -> 110 us (0.24)
  waiting for transfers between devices: 172 us -> 0 us
  matrix products: 115 us -> 0 us
  Pallas kernels: 0 us -> 103 us
  blocking collectives: 92.6 us -> 0 us
  local copies, waits for them, and re-layouts: 27.7 us -> 4.71 us
  other arithmetic: 20.9 us -> 1.27 us
  loops' own time: 16.9 us -> 0 us
  between operations: 14 us -> 0.64 us
    reduce_scatter x2 -> x0, waiting for transfers between devices: 121 us -> none  [the longest x1 73.6 us: on_device(): lax.psum_scatter(pair_grads.astype(jnp.bfloat16), 'ctx', scatter_dimensio...]
    dot_general x58 -> x0, matrix products: 115 us -> none  [the longest x16 35.2 us: scores_for(): jnp.einsum('tgrd,sgd->tgrs', queries, block_pairs[:, :, 0], preferred_ele...]
    pallas_call x0 -> x1, Pallas kernels: none -> 103 us  [on_device(): pl.pallas_call(functools.partial(kernel, n_ctx), out_shape=(jax.ShapeDtyp...]
    psum x3 -> x0, blocking collectives: 69.1 us -> none  [the longest x1 41.1 us: on_device(): grad_gain = lax.psum(jnp.sum(dnormed * features * recip, 0), 'ctx')]
    all_gather x2 -> x0, waiting for transfers between devices: 51.3 us -> none  [the longest x1 28.3 us: on_device(): lax.all_gather(dproj, 'head', axis=1, tiled=True)]
    all_gather x1 -> x0, blocking collectives: 23.5 us -> none  [on_device(): key_segment = lax.all_gather(segment, 'ctx', axis=0, tiled=True)]
    another operation x3 -> x0, loops' own time: 16.9 us -> none  [the longest x1 5.77 us: on_device(): lax.scan(stats_step, start_stats, jnp.arange(block_count, dtype=jnp.int32))]
    dynamic_slice x48 -> x0, local copies, waits for them, and re-layouts: 15.9 us -> none  [the longest x24 14 us: on_device(): lax.scan(stats_step, start_stats, jnp.arange(block_count, dtype=jnp.int32))]
  transfers between devices with their start and end apart: 4 -> 0, of which waited for: 4 -> 0; matrix products, arithmetic and copies ran while one was open for 1% -> 0% of each run, Pallas kernels for 0% -> 0%
where the time goes in v1:
time: 110 us
  Pallas kernels  103 us (94%)
  local copies, waits for them, and re-layouts  4.71 us (4%)
  other arithmetic  1.27 us (1%)
    pallas_call x1, Pallas kernels, on_device(): pl.pallas_call(functools.partial(kernel, n_ctx), out_shape=(jax.ShapeDtyp...  103 us
    unnamed x2, local copies, waits for them, and re-layouts  3.45 us

profile of v1, /device:TPU:0, one launch (start us, length us, event | category | flops | bytes accessed | tf_op | source)
XLA Modules:
  0.0 109.8 jit_solution(13918108956461675358)
XLA Ops:
  0.6 1.3 %reshape.18.gain = f32[1,640]{1,0:T(1,128)} reshape(f32[640]{0:T(1024)} %param.7) | data formatting | bytes 5120 | tf_op jit(solution)/shard_map/reshape | solution.py:502
  1.9 103.2 %shard_map.85 = (bf16[256,640]{1,0:T(8,128)(2,1)}, bf16[256,640]{1,0:T(8,128)(2,1)}, f32[1,640]{1,0:T(1,128)}) custom-call(bf16[256,640]{1,0:T(8,128)(2,1)} %tok.1, f32[1,640]{1,0:T(1,128)} %reshape.18.gain, bf16[640,7168]{1,0:T(8,128)(2,1)} %w_hbm.1, bf16[256,640]{1,0:T(8,128)(2,1)} %target.1, s32[1,256]{1,0:T(1,128)} %bitcast.2, s32[1,256]{1,0:T(1,128)} %bitcast.3), custom_call_target="tpu_custom_call" | custom-call | tf_op jit(solution)/shard_map/pallas_call | solution.py:487
  105.1 1.3 %reduce = f32[640]{0:T(1024)} reduce(f32[1,640]{1,0:T(1,128)} %get-tuple-element.8, f32[]{:T(128)} %constant), dimensions={0}, to_apply=%get-tuple-element.8.reduce_sub_computation | reduce | bytes 5124 | tf_op jit(solution)/shard_map/pallas_call | solution.py:487
  106.4 1.7 %copy.11 = bf16[256,640]{1,0:T(8,128)(2,1)} copy(bf16[256,640]{1,0:T(8,128)(2,1)} %get-tuple-element.12) | data formatting | bytes 655360
  108.1 1.7 %copy.12 = bf16[256,640]{1,0:T(8,128)(2,1)} copy(bf16[256,640]{1,0:T(8,128)(2,1)} %get-tuple-element.13) | data formatting | bytes 655360

commit v2 on v1

v2 whole, which is shorter than its diff:
```python
import functools

import jax
import jax.numpy as jnp
from jax import lax
from jax.experimental import pallas as pl
from jax.experimental.pallas import tpu as pltpu
from jax.sharding import PartitionSpec as P

D = 5120
HD = 128
HEADS = 5
WINDOW = 8
EPSILON = 1e-06
SCALE = HD**-0.5
LOG2E = 1.4426950408889634
EXP_SCALE = SCALE * LOG2E
HIDDEN = -1e30
PIECES = ((640, 256), (0, 256), (256, 384))
GROUP = 3
STEPS = (2, 1, 3, 0)
F32 = jnp.float32
BF16 = jnp.bfloat16


def kernel(
    n_ctx, tok, gain, w_hbm, target, advantage, segment,
    attn, grad_tokens, grad_gain,
    xb, wv, part_send, part_recv, chip_sum, hold, own, relay, landed, landed_far,
    stats, recip, window, key_t, value_t, bias,
    q_rows, q_t, go_t, scores, expo, out_t, gp_rows, gp_t, dq_t, pair_acc, pair_send, pair_recv,
    dproj, inner_stats, dnormed, gain_stats,
    w_sem, ps_send, ps_recv, r1_send, r1_recv, r2_send, r2_recv, st_send, st_recv,
    win_ssem, win_rsem, pair_ssem, pair_rsem,
    ag_send, ag_recv, in_send, in_recv, gg_send, gg_recv,
):
    rows, wide_in = tok.shape
    half = rows // 2
    seg_at = 2 * rows
    c = lax.axis_index("ctx")
    h = lax.axis_index("head")
    x = h // 2
    p = lax.rem(h, 2)
    z = c // 4
    y = lax.rem(c, 4)
    rings = n_ctx // 4
    up, down = z * 4 + lax.rem(y + 1, 4), z * 4 + lax.rem(y + 3, 4)

    def head_of(xx, pp):
        return lax.rem(xx + 8, 4) * 2 + pp

    right, left, partner = head_of(x + 1, p), head_of(x - 1, p), head_of(x, 1 - p)
    far = head_of(x + 2, p)
    started = []

    def remote(src, dst, send, recv, **where):
        axis, index = next(iter(where.items()))
        return pltpu.make_async_remote_copy(
            src_ref=src, dst_ref=dst, send_sem=send, recv_sem=recv,
            device_id={axis: index}, device_id_type=pl.DeviceIdType.MESH,
        )

    def start(copy, when=None):
        started.append((copy, when))
        if when is None:
            copy.start()
        else:
            pl.when(when)(copy.start)

    def arrived(dst, recv):
        remote(dst, dst, recv, recv, head=partner).wait_recv()

    barrier = pltpu.get_barrier_semaphore()
    for other in (partner, right, left, head_of(x + 2, p)):
        pl.semaphore_signal(
            barrier, inc=1, device_id={"head": other}, device_id_type=pl.DeviceIdType.MESH
        )
    others = [lax.rem(c + d, n_ctx) for d in range(1, n_ctx)]
    for other in others:
        pl.semaphore_signal(
            barrier, inc=1, device_id={"ctx": other}, device_id_type=pl.DeviceIdType.MESH
        )

    def fetch(s, i):
        off, wide = PIECES[s]
        g = head_of(x + STEPS[i % 4], (1 - p) if i < 4 else p)
        first = pl.multiple_of(g * 896 + off, 128)
        return g, pltpu.make_async_copy(
            w_hbm.at[:, pl.ds(first, wide)], wv.at[g, :, pl.ds(off, wide)], w_sem.at[s, i]
        )

    for s in range(3):
        for i in range(8):
            fetch(s, i)[1].start()

    gain_row = gain[...].reshape(1, wide_in)
    xb[...] = (tok[...].astype(F32) * gain_row).astype(BF16)

    def project(s):
        off, wide = PIECES[s]
        cols = pl.ds(off, wide)
        for i in range(4):
            g, copy = fetch(s, i)
            copy.wait()
            part_send[i, :, off : off + wide] = jnp.dot(
                xb[...], wv[g, :, off : off + wide], preferred_element_type=F32
            ).astype(BF16)
            if s == 0 and i == 0:
                pl.semaphore_wait(barrier, 4 + len(others))
            start(remote(
                part_send.at[i, :, cols], part_recv.at[i, :, cols],
                ps_send.at[s, i], ps_recv.at[s, i], head=partner,
            ))
        for i in range(4):
            g, copy = fetch(s, 4 + i)
            copy.wait()
            mine = jnp.dot(xb[...], wv[g, :, off : off + wide], preferred_element_type=F32)
            arrived(part_recv.at[i, :, cols], ps_recv.at[s, i])
            mine = mine + part_recv[i, :, off : off + wide].astype(F32)
            if i < 3:
                chip_sum[i, :, off : off + wide] = mine.astype(BF16)
            top = pl.ds(0, half)
            low = pl.ds(half, half)
            if s == 0 and i < 3:
                start(remote(
                    chip_sum.at[i, :, cols], (landed_far, landed.at[0, :, cols], landed.at[1, :, cols])[i],
                    r2_send.at[s, i], r2_recv.at[s, i], head=(far, right, left)[i],
                ))
            elif i == 0:
                start(remote(
                    chip_sum.at[0, top, cols], relay.at[0, :, cols],
                    r1_send.at[s, 0], r1_recv.at[s, 0], head=right,
                ))
                start(remote(
                    chip_sum.at[0, low, cols], relay.at[1, :, cols],
                    r1_send.at[s, 1], r1_recv.at[s, 1], head=left,
                ))
            elif i == 1:
                hold[0, :, off : off + wide] = mine[:half]
                start(remote(
                    chip_sum.at[1, low, cols], landed.at[0, low, cols],
                    r2_send.at[s, 0], r2_recv.at[s, 0], head=right,
                ))
            elif i == 2:
                hold[1, :, off : off + wide] = mine[half:]
                start(remote(
                    chip_sum.at[2, top, cols], landed.at[1, top, cols],
                    r2_send.at[s, 1], r2_recv.at[s, 1], head=left,
                ))
            else:
                own[:, off : off + wide] = mine

    def pass_on(s):
        off, wide = PIECES[s]
        cols = pl.ds(off, wide)
        top = pl.ds(0, half)
        low = pl.ds(half, half)
        arrived(relay.at[0, :, cols], r1_recv.at[s, 0])
        chip_sum[1, :half, off : off + wide] = (
            hold[0, :, off : off + wide] + relay[0, :, off : off + wide].astype(F32)
        ).astype(BF16)
        start(remote(
            chip_sum.at[1, top, cols], landed.at[0, top, cols],
            r2_send.at[s, 2], r2_recv.at[s, 2], head=right,
        ))
        arrived(relay.at[1, :, cols], r1_recv.at[s, 1])
        chip_sum[2, half:, off : off + wide] = (
            hold[1, :, off : off + wide] + relay[1, :, off : off + wide].astype(F32)
        ).astype(BF16)
        start(remote(
            chip_sum.at[2, low, cols], landed.at[1, low, cols],
            r2_send.at[s, 3], r2_recv.at[s, 3], head=left,
        ))

    def finish(s):
        off, wide = PIECES[s]
        cols = pl.ds(off, wide)
        top = pl.ds(0, half)
        low = pl.ds(half, half)
        if s == 0:
            arrived(landed_far, r2_recv.at[0, 0])
            arrived(landed.at[0, :, cols], r2_recv.at[0, 1])
            arrived(landed.at[1, :, cols], r2_recv.at[0, 2])
        else:
            arrived(landed.at[0, low, cols], r2_recv.at[s, 0])
            arrived(landed.at[1, top, cols], r2_recv.at[s, 1])
            arrived(landed.at[0, top, cols], r2_recv.at[s, 2])
            arrived(landed.at[1, low, cols], r2_recv.at[s, 3])
        total = own[:, off : off + wide] + landed[0, :, off : off + wide].astype(F32)
        total = total + landed[1, :, off : off + wide].astype(F32)
        if s == 0:
            total = total + landed_far[...].astype(F32)
        scale = recip[:, :1]
        return (total * scale).astype(BF16)

    def small_first(ref, send, recv):
        start(remote(ref.at[0], ref.at[1], send.at[0], recv.at[0], head=partner))

    def small_second(ref, send, recv):
        arrived(ref.at[1], recv.at[0])
        ref[2] = ref[0] + ref[1]
        for d in range(1, 4):
            start(remote(ref.at[2], ref.at[2 + d], send.at[d], recv.at[d], head=head_of(x + d, p)))

    def small_total(ref, recv):
        for d in range(1, 4):
            arrived(ref.at[2 + d], recv.at[d])
        return jnp.transpose(ref[2] + ref[3] + ref[4] + ref[5])[:, :1]

    project(0)
    features = tok[...].astype(F32)
    stats[0] = lax.dot_general(
        jnp.ones((8, wide_in), F32), features * features, (((1,), (1,)), ((), ())),
        precision=lax.Precision.HIGHEST, preferred_element_type=F32,
    )
    small_first(stats, st_send, st_recv)
    seg_row = segment[...].astype(F32)
    which = lax.broadcasted_iota(jnp.int32, (16, HD), 0)
    seg_block = jnp.zeros((16, HD), F32)
    for k in range(rows // HD):
        seg_block = jnp.where(which == k, seg_row[:, k * HD : (k + 1) * HD], seg_block)
    window[0, seg_at:] = seg_block.astype(BF16)
    small_second(stats, st_send, st_recv)
    project(1)
    recip[...] = jnp.broadcast_to(
        lax.rsqrt(small_total(stats, st_recv) / D + EPSILON), (rows, HD)
    )

    pair = finish(0)
    window[0, :rows] = pair[:, :HD]
    window[0, rows:seg_at] = pair[:, HD:]

    def share(n, src, dst, to, when):
        start(remote(window.at[src], window.at[dst], win_ssem.at[n], win_rsem.at[dst], ctx=to), when)

    def here(j):
        pl.when(c >= j)(lambda: arrived(window.at[j], win_rsem.at[j]))

    def share_first():
        for d in (1, 2):
            share(d, 0, 4 * d, jnp.minimum(c + 4 * d, n_ctx - 1), z + d < rings)
        for d in range(1, 4):
            share(2 + d, 0, d, z * 4 + jnp.minimum(y + d, 3), y + d <= 3)

    def share_second():
        here(4)
        for d in (1, 3, 2):
            share(5 + d, 4, 4 + d - 4 * ((y + d) // 4), z * 4 + lax.rem(y + d, 4), z >= 1)

    def share_third():
        here(8)
        for d in range(1, 4):
            share(8 + d, 8, 8 - d, z * 4 + jnp.maximum(y - d, 0), (z >= 2) & (y >= d))

    def share_last():
        for j in (1, 2, 3, 5, 6, 7):
            here(j)

    share_first()
    pass_on(1)
    project(2)
    share_second()
    pass_on(2)

    factor = 0.25 * advantage[...].astype(F32)
    for r in range(HEADS):
        block = jnp.transpose(target[:, r * HD : (r + 1) * HD].astype(F32))
        go_t[:, r * rows : (r + 1) * rows] = (block * factor).astype(BF16)

    def queries(s):
        q = finish(s)
        first = PIECES[s][0] // HD
        for i in range(PIECES[s][1] // HD):
            one = q[:, i * HD : (i + 1) * HD]
            q_rows[(first + i) * rows : (first + i + 1) * rows] = one
            q_t[:, (first + i) * rows : (first + i + 1) * rows] = jnp.transpose(one.astype(F32)).astype(BF16)

    share_third()
    queries(1)
    share_last()

    blocks = jnp.minimum(c, WINDOW) + 1
    groups = (blocks + GROUP - 1) // GROUP

    def prepare(j, diagonal):
        span = pl.ds(pl.multiple_of(j * rows, rows), rows)
        key_t[:, span] = jnp.transpose(window[j, :rows].astype(F32)).astype(BF16)
        value_t[:, span] = jnp.transpose(window[j, rows:seg_at].astype(F32)).astype(BF16)
        ids = jnp.transpose(window[j, seg_at:].astype(F32))
        for k in range(rows // HD):
            visible = ids[:, k : k + 1] == seg_row
            if diagonal:
                k_pos = lax.broadcasted_iota(jnp.int32, (HD, rows), 0) + k * HD
                q_pos = lax.broadcasted_iota(jnp.int32, (HD, rows), 1)
                visible = visible & (k_pos <= q_pos)
            bias[j, k * HD : (k + 1) * HD] = jnp.where(visible, 0.0, HIDDEN)

    prepare(0, True)

    @pl.loop(1, blocks)
    def _(j):
        prepare(j, False)

    @pl.loop(blocks, groups * GROUP)
    def _(j):
        span = pl.ds(pl.multiple_of(j * rows, rows), rows)
        window[j] = jnp.zeros((seg_at + 16, HD), BF16)
        key_t[:, span] = jnp.zeros((HD, rows), BF16)
        value_t[:, span] = jnp.zeros((HD, rows), BF16)
        bias[j] = jnp.full((rows, rows), HIDDEN, F32)

    def forward(s):
        off, wide = PIECES[s]
        heads = wide // HD
        n = heads * rows
        first = off // HD * rows
        span = slice(first, first + n)

        def score_group(g, top):
            for u in range(GROUP):
                j = g * GROUP + u
                block = jnp.dot(window[j, :rows], q_t[:, span], preferred_element_type=F32)
                block = block + jnp.concatenate([bias[j]] * heads, axis=1)
                scores[j, :, :n] = block
                top = jnp.maximum(top, jnp.max(block.reshape(rows // 8, 8, n), 0))
            return top

        top = lax.fori_loop(0, groups, score_group, jnp.full((8, n), HIDDEN, F32))
        top = jnp.max(top, 0, keepdims=True) * EXP_SCALE
        out_t[:, :n] = jnp.zeros((HD, n), F32)

        def expo_group(g, total):
            ebs = []
            for u in range(GROUP):
                j = g * GROUP + u
                e = jnp.exp2(scores[j, :, :n] * EXP_SCALE - top)
                eb = e.astype(BF16)
                expo[j, :, :n] = eb
                ebs.append(eb)
                total = total + jnp.sum(e.reshape(rows // 8, 8, n), 0)
            keys = pl.ds(pl.multiple_of(g * GROUP * rows, rows), GROUP * rows)
            out_t[:, :n] += jnp.dot(
                value_t[:, keys], jnp.concatenate(ebs, axis=0), preferred_element_type=F32
            )
            return total

        total = lax.fori_loop(0, groups, expo_group, jnp.zeros((8, n), F32))
        inverse = 1.0 / jnp.sum(total, 0, keepdims=True)
        out_b = (out_t[:, :n] * inverse).astype(BF16).astype(F32)
        go = go_t[:, span].astype(F32)
        delta = jnp.sum(go * out_b, 0, keepdims=True) * inverse
        scaled = go * inverse
        gp_t[:, :n] = scaled.astype(BF16)
        for i in range(heads):
            r = off // HD + i
            attn[:, r * HD : (r + 1) * HD] = jnp.transpose(out_b[:, i * rows : (i + 1) * rows]).astype(BF16)
            gp_rows[i * rows : (i + 1) * rows] = jnp.transpose(scaled[:, i * rows : (i + 1) * rows]).astype(BF16)
        return delta

    def give(j, to, when):
        start(remote(pair_send.at[j], pair_recv.at[j], pair_ssem.at[j], pair_rsem.at[j], ctx=to), when)

    def take(j, into, when):
        def add_in():
            arrived(pair_recv.at[j], pair_rsem.at[j])
            pair_acc[into] += pair_recv[j].astype(F32)

        pl.when(when)(add_in)

    def give_sum(j):
        def store():
            pair_send[j] = pair_acc[j].astype(BF16)

        pl.when(c >= j)(store)
        give(j, jnp.maximum(c - j, 0), c >= j)

    def after_group(g):
        for j in reversed(range(g * GROUP, (g + 1) * GROUP)):
            if j % 4:
                give(j, z * 4 + lax.rem(y + 8 - j, 4), c >= j)

    def pair_second():
        for j in (7, 6, 5, 3, 2, 1):
            take(j, 4 * ((y + j) // 4), z * 4 + lax.rem(y + j, 4) >= j)
            if j == 5:
                give_sum(8)
        give_sum(4)

    def pair_third():
        for j in (8, 4):
            take(j, 0, z + j // 4 < rings)

    def backward(s, delta, last):
        off, wide = PIECES[s]
        heads = wide // HD
        n = heads * rows
        first = off // HD * rows
        span = slice(first, first + n)
        dq_t[:, :n] = jnp.zeros((HD, n), F32)

        def group(g):
            all_ds = []
            for u in reversed(range(GROUP)):
                j = g * GROUP + u
                dp = jnp.dot(window[j, rows:seg_at], gp_t[:, :n], preferred_element_type=F32)
                eb = expo[j, :, :n]
                ds = (eb.astype(F32) * (dp - delta)).astype(BF16)
                all_ds.insert(0, ds)
                dk = jnp.dot(ds, q_rows[span], preferred_element_type=F32) * SCALE
                dv = jnp.dot(eb, gp_rows[:n], preferred_element_type=F32)
                if not last:
                    pair_acc[j, :, :HD] = dk
                    pair_acc[j, :, HD:] = dv
                else:
                    dk = dk + pair_acc[j, :, :HD]
                    dv = dv + pair_acc[j, :, HD:]
                    if j % 4 == 0:
                        pair_acc[j, :, :HD] = dk
                        pair_acc[j, :, HD:] = dv
                    else:
                        pair_send[j, :, :HD] = dk.astype(BF16)
                        pair_send[j, :, HD:] = dv.astype(BF16)
            keys = pl.ds(pl.multiple_of(g * GROUP * rows, rows), GROUP * rows)
            dq_t[:, :n] += jnp.dot(
                key_t[:, keys], jnp.concatenate(all_ds, axis=0), preferred_element_type=F32
            )

        if last:
            for g in reversed(range(WINDOW // GROUP + 1)):
                pl.when(g < groups)(functools.partial(group, g))
                after_group(g)
        else:
            pl.loop(0, groups)(group)

        inner = jnp.zeros((1, rows), F32)
        for i in range(heads):
            r = off // HD + i
            one = dq_t[:, i * rows : (i + 1) * rows] * SCALE
            dproj[h, :, r * HD : (r + 1) * HD] = jnp.transpose(one).astype(BF16)
            inner += jnp.sum(one * q_t[:, r * rows : (r + 1) * rows].astype(F32), 0, keepdims=True)
        return inner

    def slot(ref, s, who, lo, size):
        off, wide = PIECES[s]
        return ref.at[who, pl.ds(lo, size), pl.ds(off, wide)]

    def move(s, n, who, lo, size, to):
        start(remote(slot(dproj, s, who, lo, size), slot(dproj, s, who, lo, size),
                     ag_send.at[s, n], ag_recv.at[s, n], head=to))

    def landed_piece(s, n, who, lo, size):
        arrived(slot(dproj, s, who, lo, size), ag_recv.at[s, n])

    def gather_send(s):
        for n, to in enumerate((right, left, far, partner)):
            move(s, n, h, 0, rows, to)

    def gather_pass(s):
        for n, who in enumerate((left, right, far)):
            landed_piece(s, n, who, 0, rows)
            move(s, 4 + n, who, 0, rows, partner)

    def add(s, who, fresh=False):
        off, wide = PIECES[s]
        value = lax.dot_general(
            dproj[who, :, off : off + wide], wv[who, :, off : off + wide],
            (((1,), (1,)), ((), ())), preferred_element_type=F32,
        )
        if fresh:
            dnormed[...] = value
        else:
            dnormed[...] += value

    def add_own(s, fresh=False):
        add(s, h, fresh)
        for who in (left, right, far):
            add(s, who)

    def add_rest(s):
        landed_piece(s, 3, partner, 0, rows)
        add(s, partner)
        for n, d in enumerate((3, 1, 2)):
            who = head_of(x + d, 1 - p)
            landed_piece(s, 4 + n, who, 0, rows)
            add(s, who)

    delta = forward(1)
    inner = backward(1, delta, False)
    gather_send(1)
    queries(2)
    delta = forward(2)
    inner += backward(2, delta, True)
    gather_send(2)
    gather_pass(1)
    add_own(1, True)
    pair_second()
    add_rest(1)
    gather_pass(2)
    pair_third()

    pair_grad = pair_acc[0]
    dproj[h, :, PIECES[0][0] :] = pair_grad.astype(BF16)
    gather_send(0)
    prod = pair_grad[:, :HD] * window[0, :rows].astype(F32) + pair_grad[:, HD:] * window[0, rows:seg_at].astype(F32)
    inner += jnp.sum(jnp.transpose(prod), 0, keepdims=True)
    inner_stats[0] = jnp.broadcast_to(inner, (8, rows))
    small_first(inner_stats, in_send, in_recv)
    add_own(2)
    small_second(inner_stats, in_send, in_recv)
    gather_pass(0)
    add_rest(2)
    add_own(0)
    inner_col = small_total(inner_stats, in_recv)
    add_rest(0)

    scale = recip[:, :1]
    weighted = tok[...].astype(F32) * scale
    gain_part = jnp.sum(dnormed[...] * weighted, 0, keepdims=True)
    lanes = wide_in // 128
    gain_stats[0] = jnp.zeros((8, 128), F32)
    for k in range(lanes):
        gain_stats[0, k : k + 1] = gain_part[:, k * 128 : (k + 1) * 128]
    for d in range(1, n_ctx):
        start(remote(
            gain_stats.at[0], gain_stats.at[d], gg_send.at[d], gg_recv.at[d], ctx=lax.rem(c + d, n_ctx),
        ))
    grad_tokens[...] = (
        dnormed[...] * gain[...].reshape(1, wide_in) * scale - weighted * (scale * inner_col * (1.0 / D))
    ).astype(BF16)
    gain_total = gain_stats[0]
    for d in range(1, n_ctx):
        arrived(gain_stats.at[d], gg_recv.at[d])
        gain_total = gain_total + gain_stats[d]
    grad_gain[...] = gain_total

    for copy, when in started:
        if when is None:
            copy.wait_send()
        else:
            pl.when(when)(copy.wait_send)


def hand_over(attn, grad_tokens, gain_rows, attn_out, grad_out, gain_out):
    attn_out[...] = attn[...]
    grad_out[...] = grad_tokens[...]
    wide = gain_out.shape[0]
    gain_out[...] = gain_rows[: wide // 128].reshape(wide)


def on_device(n_ctx, tokens, gain, qkv_weight, target, advantage, segment):
    rows, wide = tokens.shape
    group = qkv_weight.shape[1] // 8
    n = 3 * rows
    slots = WINDOW + 1
    vmem = pl.BlockSpec(memory_space=pltpu.VMEM)
    anywhere = pl.BlockSpec(memory_space=pl.ANY)
    scratch = [
        ((rows, wide), BF16), ((8, wide, group), BF16),
        ((4, rows, group), BF16), ((4, rows, group), BF16), ((3, rows, group), BF16),
        ((2, rows // 2, group), F32), ((rows, group), F32),
        ((2, rows // 2, group), BF16), ((2, rows, group), BF16), ((rows, 2 * HD), BF16),
        ((6, 8, rows), F32), ((rows, HD), F32), ((slots, 2 * rows + 16, HD), BF16),
        ((HD, slots * rows), BF16), ((HD, slots * rows), BF16), ((slots, rows, rows), F32),
        ((HEADS * rows, HD), BF16), ((HD, HEADS * rows), BF16), ((HD, HEADS * rows), BF16),
        ((slots, rows, n), F32), ((slots, rows, n), BF16), ((HD, n), F32),
        ((n, HD), BF16), ((HD, n), BF16), ((HD, n), F32),
        ((slots, rows, 2 * HD), F32), ((slots, rows, 2 * HD), BF16), ((slots, rows, 2 * HD), BF16),
        ((8, rows, group), BF16), ((6, 8, rows), F32), ((rows, wide), F32), ((n_ctx, 8, 128), F32),
    ]
    sems = [
        (3, 8), (3, 4), (3, 4), (3, 2), (3, 2), (3, 4), (3, 4), (4,), (4,),
        (12,), (slots,), (slots,), (slots,),
        (3, 7), (3, 7), (4,), (4,), (n_ctx,), (n_ctx,),
    ]
    out_types = (
        jax.ShapeDtypeStruct((rows, HEADS * HD), BF16),
        jax.ShapeDtypeStruct((rows, wide), BF16),
    )
    out, grad_tokens, gain_rows = pl.pallas_call(
        functools.partial(kernel, n_ctx),
        out_shape=(*out_types, jax.ShapeDtypeStruct((8, 128), F32)),
        in_specs=[vmem, vmem, anywhere, vmem, vmem, vmem],
        out_specs=(vmem, vmem, vmem),
        scratch_shapes=[pltpu.VMEM(shape, dtype) for shape, dtype in scratch]
        + [pltpu.SemaphoreType.DMA(shape) for shape in sems],
        compiler_params=pltpu.CompilerParams(
            collective_id=0, has_side_effects=True, vmem_limit_bytes=60 * 1024 * 1024
        ),
    )(
        tokens, gain, qkv_weight, target,
        advantage.reshape(1, rows), segment.reshape(1, rows),
    )
    return pl.pallas_call(
        hand_over,
        out_shape=(*out_types, jax.ShapeDtypeStruct((wide,), F32)),
        in_specs=[vmem, vmem, vmem],
        out_specs=(vmem, vmem, vmem),
    )(out, grad_tokens, gain_rows)


def solution(mesh):
    placed = (P("ctx", "head"), P("head"), P("head", None), P("ctx", "head"), P("ctx"), P("ctx"))
    return jax.shard_map(
        functools.partial(on_device, mesh.shape["ctx"]),
        mesh=mesh,
        in_specs=placed,
        out_specs=(P("ctx", "head"), P("ctx", "head"), P("head")),
        check_vma=False,
    )
```

time: 110 us -> 90.5 us (0.82)
  Pallas kernels: 103 us -> 89.7 us
  local copies, waits for them, and re-layouts: 4.71 us -> 0 us
  other arithmetic: 1.27 us -> 0 us
    pallas_call x1 -> x2, Pallas kernels: 103 us -> 89.7 us  [the longest x1 87.8 us: on_device(): pl.pallas_call(functools.partial(kernel, n_ctx), out_shape=(*out_types, j...]
    unnamed x2 -> x0, local copies, waits for them, and re-layouts: 3.45 us -> none
    pallas_call x1 -> x0, other arithmetic: 1.27 us -> none  [on_device(): pl.pallas_call(functools.partial(kernel, n_ctx), out_shape=(jax.ShapeDtyp...]
    reshape x1 -> x0, local copies, waits for them, and re-layouts: 1.27 us -> none  [on_device(): gain.reshape(1, wide)]
where the time goes in v2:
time: 90.5 us; the launch traced here: 90.4 us
  Pallas kernels  89.7 us (99%)
    pallas_call x1, Pallas kernels, on_device(): pl.pallas_call(functools.partial(kernel, n_ctx), out_shape=(*out_types, j...  87.8 us
    pallas_call x1, Pallas kernels, on_device(): pl.pallas_call(hand_over, out_shape=(*out_types, jax.ShapeDtypeStruct((wi...  1.94 us

profile of v2, /device:TPU:0, one launch (start us, length us, event | category | flops | bytes accessed | tf_op | source)
XLA Modules:
  0.0 90.4 jit_solution(2926103014912769446)
XLA Ops:
  0.6 87.8 %shard_map.85 = (bf16[256,640]{1,0:T(8,128)(2,1)}, bf16[256,640]{1,0:T(8,128)(2,1)}, f32[8,128]{1,0:T(8,128)}) custom-call(bf16[256,640]{1,0:T(8,128)(2,1)} %tok.1, f32[640]{0:T(1024)} %gain.1, bf16[640,7168]{1,0:T(8,128)(2,1)} %w_hbm.1, bf16[256,640]{1,0:T(8,128)(2,1)} %target.1, s32[1,256]{1,0:T(1,128)} %bitcast.2, s32[1,256]{1,0:T(1,128)} %bitcast.3), custom_call_target="tpu_custom_call" | custom-call | tf_op jit(solution)/shard_map/pallas_call | solution.py:579
  88.4 1.9 %shard_map.86 = (bf16[256,640]{1,0:T(8,128)(2,1)}, bf16[256,640]{1,0:T(8,128)(2,1)}, f32[640]{0:T(1024)}) custom-call(bf16[256,640]{1,0:T(8,128)(2,1)} %get-tuple-element.6.attn, bf16[256,640]{1,0:T(8,128)(2,1)} %get-tuple-element.7.grad_tokens, f32[8,128]{1,0:T(8,128)} %get-tuple-element.8.gain_rows), custom_call_target="tpu_custom_call" | custom-call | tf_op jit(solution)/shard_map/pallas_call | solution.py:593

commit v3 on v2

--- a/solution.py
+++ b/solution.py
@@ -16,7 +16,8 @@
 LOG2E = 1.4426950408889634
 EXP_SCALE = SCALE * LOG2E
 HIDDEN = -1e30
-PIECES = ((640, 256), (0, 256), (256, 384))
+PIECES = ((640, 128), (768, 128), (0, 256), (256, 384))
+KEYS, VALUES, FIRST, SECOND = range(4)
 GROUP = 3
 STEPS = (2, 1, 3, 0)
 F32 = jnp.float32
@@ -27,7 +28,7 @@
     n_ctx, tok, gain, w_hbm, target, advantage, segment,
     attn, grad_tokens, grad_gain,
     xb, wv, part_send, part_recv, chip_sum, hold, own, relay, landed, landed_far,
-    stats, recip, window, key_t, value_t, bias,
+    stats, recip, key_win, value_win, key_t, value_t, bias,
     q_rows, q_t, go_t, scores, expo, out_t, gp_rows, gp_t, dq_t, pair_acc, pair_send, pair_recv,
     dproj, inner_stats, dnormed, gain_stats,
     w_sem, ps_send, ps_recv, r1_send, r1_recv, r2_send, r2_recv, st_send, st_recv,
@@ -36,7 +37,6 @@
 ):
     rows, wide_in = tok.shape
     half = rows // 2
-    seg_at = 2 * rows
     c = lax.axis_index("ctx")
     h = lax.axis_index("head")
     x = h // 2
@@ -89,7 +89,7 @@
             w_hbm.at[:, pl.ds(first, wide)], wv.at[g, :, pl.ds(off, wide)], w_sem.at[s, i]
         )
 
-    for s in range(3):
+    for s in range(4):
         for i in range(8):
             fetch(s, i)[1].start()
 
@@ -121,9 +121,9 @@
                 chip_sum[i, :, off : off + wide] = mine.astype(BF16)
             top = pl.ds(0, half)
             low = pl.ds(half, half)
-            if s == 0 and i < 3:
+            if s < 2 and i < 3:
                 start(remote(
-                    chip_sum.at[i, :, cols], (landed_far, landed.at[0, :, cols], landed.at[1, :, cols])[i],
+                    chip_sum.at[i, :, cols], (landed_far.at[s], landed.at[0, :, cols], landed.at[1, :, cols])[i],
                     r2_send.at[s, i], r2_recv.at[s, i], head=(far, right, left)[i],
                 ))
             elif i == 0:
@@ -177,10 +177,10 @@
         cols = pl.ds(off, wide)
         top = pl.ds(0, half)
         low = pl.ds(half, half)
-        if s == 0:
-            arrived(landed_far, r2_recv.at[0, 0])
-            arrived(landed.at[0, :, cols], r2_recv.at[0, 1])
-            arrived(landed.at[1, :, cols], r2_recv.at[0, 2])
+        if s < 2:
+            arrived(landed_far.at[s], r2_recv.at[s, 0])
+            arrived(landed.at[0, :, cols], r2_recv.at[s, 1])
+            arrived(landed.at[1, :, cols], r2_recv.at[s, 2])
         else:
             arrived(landed.at[0, low, cols], r2_recv.at[s, 0])
             arrived(landed.at[1, top, cols], r2_recv.at[s, 1])
@@ -188,8 +188,8 @@
             arrived(landed.at[1, low, cols], r2_recv.at[s, 3])
         total = own[:, off : off + wide] + landed[0, :, off : off + wide].astype(F32)
         total = total + landed[1, :, off : off + wide].astype(F32)
-        if s == 0:
-            total = total + landed_far[...].astype(F32)
+        if s < 2:
+            total = total + landed_far[s].astype(F32)
         scale = recip[:, :1]
         return (total * scale).astype(BF16)
 
@@ -207,60 +207,67 @@
             arrived(ref.at[2 + d], recv.at[d])
         return jnp.transpose(ref[2] + ref[3] + ref[4] + ref[5])[:, :1]
 
-    project(0)
+    project(KEYS)
     features = tok[...].astype(F32)
     stats[0] = lax.dot_general(
         jnp.ones((8, wide_in), F32), features * features, (((1,), (1,)), ((), ())),
         precision=lax.Precision.HIGHEST, preferred_element_type=F32,
     )
     small_first(stats, st_send, st_recv)
+    project(VALUES)
+    small_second(stats, st_send, st_recv)
     seg_row = segment[...].astype(F32)
     which = lax.broadcasted_iota(jnp.int32, (16, HD), 0)
     seg_block = jnp.zeros((16, HD), F32)
     for k in range(rows // HD):
         seg_block = jnp.where(which == k, seg_row[:, k * HD : (k + 1) * HD], seg_block)
-    window[0, seg_at:] = seg_block.astype(BF16)
-    small_second(stats, st_send, st_recv)
-    project(1)
+    key_win[0, rows:] = seg_block.astype(BF16)
+    project(FIRST)
     recip[...] = jnp.broadcast_to(
         lax.rsqrt(small_total(stats, st_recv) / D + EPSILON), (rows, HD)
     )
 
-    pair = finish(0)
-    window[0, :rows] = pair[:, :HD]
-    window[0, rows:seg_at] = pair[:, HD:]
-
-    def share(n, src, dst, to, when):
-        start(remote(window.at[src], window.at[dst], win_ssem.at[n], win_rsem.at[dst], ctx=to), when)
-
-    def here(j):
-        pl.when(c >= j)(lambda: arrived(window.at[j], win_rsem.at[j]))
-
-    def share_first():
+    windows = (key_win, value_win)
+
+    def share(w, n, src, dst, to, when):
+        start(remote(
+            windows[w].at[src], windows[w].at[dst], win_ssem.at[w, n], win_rsem.at[w, dst], ctx=to,
+        ), when)
+
+    def here(w, j):
+        pl.when(c >= j)(lambda: arrived(windows[w].at[j], win_rsem.at[w, j]))
+
+    def share_first(w):
         for d in (1, 2):
-            share(d, 0, 4 * d, jnp.minimum(c + 4 * d, n_ctx - 1), z + d < rings)
+            share(w, d, 0, 4 * d, jnp.minimum(c + 4 * d, n_ctx - 1), z + d < rings)
         for d in range(1, 4):
-            share(2 + d, 0, d, z * 4 + jnp.minimum(y + d, 3), y + d <= 3)
-
-    def share_second():
-        here(4)
+            share(w, 2 + d, 0, d, z * 4 + jnp.minimum(y + d, 3), y + d <= 3)
+
+    def share_second(w):
+        here(w, 4)
         for d in (1, 3, 2):
-            share(5 + d, 4, 4 + d - 4 * ((y + d) // 4), z * 4 + lax.rem(y + d, 4), z >= 1)
-
-    def share_third():
-        here(8)
+            share(w, 5 + d, 4, 4 + d - 4 * ((y + d) // 4), z * 4 + lax.rem(y + d, 4), z >= 1)
+
+    def share_third(w):
+        here(w, 8)
         for d in range(1, 4):
-            share(8 + d, 8, 8 - d, z * 4 + jnp.maximum(y - d, 0), (z >= 2) & (y >= d))
-
-    def share_last():
+            share(w, 8 + d, 8, 8 - d, z * 4 + jnp.maximum(y - d, 0), (z >= 2) & (y >= d))
+
+    def share_last(w):
         for j in (1, 2, 3, 5, 6, 7):
-            here(j)
-
-    share_first()
-    pass_on(1)
-    project(2)
-    share_second()
-    pass_on(2)
+            here(w, j)
+
+    key_win[0, :rows] = finish(KEYS)
+    share_first(0)
+    project(SECOND)
+    value_win[0] = finish(VALUES)
+    share_first(1)
+    pass_on(FIRST)
+    share_second(0)
+    share_third(0)
+    share_second(1)
+    share_third(1)
+    pass_on(SECOND)
 
     factor = 0.25 * advantage[...].astype(F32)
     for r in range(HEADS):
@@ -275,18 +282,17 @@
             q_rows[(first + i) * rows : (first + i + 1) * rows] = one
             q_t[:, (first + i) * rows : (first + i + 1) * rows] = jnp.transpose(one.astype(F32)).astype(BF16)
 
-    share_third()
-    queries(1)
-    share_last()
+    queries(FIRST)
+    share_last(0)
 
     blocks = jnp.minimum(c, WINDOW) + 1
     groups = (blocks + GROUP - 1) // GROUP
 
-    def prepare(j, diagonal):
-        span = pl.ds(pl.multiple_of(j * rows, rows), rows)
-        key_t[:, span] = jnp.transpose(window[j, :rows].astype(F32)).astype(BF16)
-        value_t[:, span] = jnp.transpose(window[j, rows:seg_at].astype(F32)).astype(BF16)
-        ids = jnp.transpose(window[j, seg_at:].astype(F32))
+    def prepare_keys(j, diagonal):
+        key_t[:, pl.ds(pl.multiple_of(j * rows, rows), rows)] = (
+            jnp.transpose(key_win[j, :rows].astype(F32)).astype(BF16)
+        )
+        ids = jnp.transpose(key_win[j, rows:].astype(F32))
         for k in range(rows // HD):
             visible = ids[:, k : k + 1] == seg_row
             if diagonal:
@@ -295,47 +301,58 @@
                 visible = visible & (k_pos <= q_pos)
             bias[j, k * HD : (k + 1) * HD] = jnp.where(visible, 0.0, HIDDEN)
 
-    prepare(0, True)
+    prepare_keys(0, True)
 
     @pl.loop(1, blocks)
     def _(j):
-        prepare(j, False)
+        prepare_keys(j, False)
 
     @pl.loop(blocks, groups * GROUP)
     def _(j):
         span = pl.ds(pl.multiple_of(j * rows, rows), rows)
-        window[j] = jnp.zeros((seg_at + 16, HD), BF16)
+        key_win[j] = jnp.zeros((rows + 16, HD), BF16)
+        value_win[j] = jnp.zeros((rows, HD), BF16)
         key_t[:, span] = jnp.zeros((HD, rows), BF16)
-        value_t[:, span] = jnp.zeros((HD, rows), BF16)
         bias[j] = jnp.full((rows, rows), HIDDEN, F32)
 
-    def forward(s):
+    def prepare_values():
+        @pl.loop(0, groups * GROUP)
+        def _(j):
+            value_t[:, pl.ds(pl.multiple_of(j * rows, rows), rows)] = (
+                jnp.transpose(value_win[j].astype(F32)).astype(BF16)
+            )
+
+    def part(s):
         off, wide = PIECES[s]
         heads = wide // HD
-        n = heads * rows
-        first = off // HD * rows
-        span = slice(first, first + n)
+        return off // HD, heads, pl.ds(off // HD * rows, heads * rows), heads * rows
+
+    def score(s):
+        _, heads, span, n = part(s)
 
         def score_group(g, top):
             for u in range(GROUP):
                 j = g * GROUP + u
-                block = jnp.dot(window[j, :rows], q_t[:, span], preferred_element_type=F32)
+                block = jnp.dot(key_win[j, :rows], q_t[:, span], preferred_element_type=F32)
                 block = block + jnp.concatenate([bias[j]] * heads, axis=1)
-                scores[j, :, :n] = block
+                scores[j, :, span] = block
                 top = jnp.maximum(top, jnp.max(block.reshape(rows // 8, 8, n), 0))
             return top
 
         top = lax.fori_loop(0, groups, score_group, jnp.full((8, n), HIDDEN, F32))
-        top = jnp.max(top, 0, keepdims=True) * EXP_SCALE
+        return jnp.max(top, 0, keepdims=True) * EXP_SCALE
+
+    def output(s, top):
+        first, heads, span, n = part(s)
         out_t[:, :n] = jnp.zeros((HD, n), F32)
 
         def expo_group(g, total):
             ebs = []
             for u in range(GROUP):
                 j = g * GROUP + u
-                e = jnp.exp2(scores[j, :, :n] * EXP_SCALE - top)
+                e = jnp.exp2(scores[j, :, span] * EXP_SCALE - top)
                 eb = e.astype(BF16)
-                expo[j, :, :n] = eb
+                expo[j, :, span] = eb
                 ebs.append(eb)
                 total = total + jnp.sum(e.reshape(rows // 8, 8, n), 0)
             keys = pl.ds(pl.multiple_of(g * GROUP * rows, rows), GROUP * rows)
@@ -350,91 +367,99 @@
         go = go_t[:, span].astype(F32)
         delta = jnp.sum(go * out_b, 0, keepdims=True) * inverse
         scaled = go * inverse
-        gp_t[:, :n] = scaled.astype(BF16)
+        gp_t[:, span] = scaled.astype(BF16)
         for i in range(heads):
-            r = off // HD + i
+            r = first + i
             attn[:, r * HD : (r + 1) * HD] = jnp.transpose(out_b[:, i * rows : (i + 1) * rows]).astype(BF16)
-            gp_rows[i * rows : (i + 1) * rows] = jnp.transpose(scaled[:, i * rows : (i + 1) * rows]).astype(BF16)
+            gp_rows[r * rows : (r + 1) * rows] = jnp.transpose(scaled[:, i * rows : (i + 1) * rows]).astype(BF16)
         return delta
 
-    def give(j, to, when):
-        start(remote(pair_send.at[j], pair_recv.at[j], pair_ssem.at[j], pair_rsem.at[j], ctx=to), when)
-
-    def take(j, into, when):
+    def give(w, j, to, when):
+        start(remote(
+            pair_send.at[w, j], pair_recv.at[w, j], pair_ssem.at[w, j], pair_rsem.at[w, j], ctx=to,
+        ), when)
+
+    def take(w, j, into, when):
         def add_in():
-            arrived(pair_recv.at[j], pair_rsem.at[j])
-            pair_acc[into] += pair_recv[j].astype(F32)
+            arrived(pair_recv.at[w, j], pair_rsem.at[w, j])
+            pair_acc[w, into] += pair_recv[w, j].astype(F32)
 
         pl.when(when)(add_in)
 
-    def give_sum(j):
+    def give_sum(w, j):
         def store():
-            pair_send[j] = pair_acc[j].astype(BF16)
+            pair_send[w, j] = pair_acc[w, j].astype(BF16)
 
         pl.when(c >= j)(store)
-        give(j, jnp.maximum(c - j, 0), c >= j)
-
-    def after_group(g):
+        give(w, j, jnp.maximum(c - j, 0), c >= j)
+
+    def keep(w, j, value):
+        if j % 4 == 0:
+            pair_acc[w, j // 4 * 4] = value
+        else:
+            pair_send[w, j] = value.astype(BF16)
+
+    def after_group(w, g):
         for j in reversed(range(g * GROUP, (g + 1) * GROUP)):
             if j % 4:
-                give(j, z * 4 + lax.rem(y + 8 - j, 4), c >= j)
-
-    def pair_second():
+                give(w, j, z * 4 + lax.rem(y + 8 - j, 4), c >= j)
+
+    def pair_second(w):
         for j in (7, 6, 5, 3, 2, 1):
-            take(j, 4 * ((y + j) // 4), z * 4 + lax.rem(y + j, 4) >= j)
+            take(w, j, 4 * ((y + j) // 4), z * 4 + lax.rem(y + j, 4) >= j)
             if j == 5:
-                give_sum(8)
-        give_sum(4)
-
-    def pair_third():
+                give_sum(w, 8)
+        give_sum(w, 4)
+
+    def pair_third(w):
         for j in (8, 4):
-            take(j, 0, z + j // 4 < rings)
-
-    def backward(s, delta, last):
-        off, wide = PIECES[s]
-        heads = wide // HD
-        n = heads * rows
-        first = off // HD * rows
-        span = slice(first, first + n)
-        dq_t[:, :n] = jnp.zeros((HD, n), F32)
-
+            take(w, j, 0, z + j // 4 < rings)
+
+    def backward_values():
         def group(g):
-            all_ds = []
             for u in reversed(range(GROUP)):
                 j = g * GROUP + u
-                dp = jnp.dot(window[j, rows:seg_at], gp_t[:, :n], preferred_element_type=F32)
-                eb = expo[j, :, :n]
-                ds = (eb.astype(F32) * (dp - delta)).astype(BF16)
-                all_ds.insert(0, ds)
-                dk = jnp.dot(ds, q_rows[span], preferred_element_type=F32) * SCALE
-                dv = jnp.dot(eb, gp_rows[:n], preferred_element_type=F32)
-                if not last:
-                    pair_acc[j, :, :HD] = dk
-                    pair_acc[j, :, HD:] = dv
-                else:
-                    dk = dk + pair_acc[j, :, :HD]
-                    dv = dv + pair_acc[j, :, HD:]
-                    if j % 4 == 0:
-                        pair_acc[j, :, :HD] = dk
-                        pair_acc[j, :, HD:] = dv
-                    else:
-                        pair_send[j, :, :HD] = dk.astype(BF16)
-                        pair_send[j, :, HD:] = dv.astype(BF16)
+                keep(1, j, jnp.dot(expo[j], gp_rows[...], preferred_element_type=F32))
+
+        for g in reversed(range(WINDOW // GROUP + 1)):
+            pl.when(g < groups)(functools.partial(group, g))
+            after_group(1, g)
+
+    def score_gradients(s, j, delta):
+        _, _, span, _ = part(s)
+        dp = jnp.dot(value_win[j], gp_t[:, span], preferred_element_type=F32)
+        expo[j, :, span] = (expo[j, :, span].astype(F32) * (dp - delta)).astype(BF16)
+
+    def backward_first(delta):
+        @pl.loop(0, groups)
+        def _(g):
+            for u in range(GROUP):
+                score_gradients(FIRST, g * GROUP + u, delta)
+
+    def backward_keys(delta):
+        def group(g):
+            for u in reversed(range(GROUP)):
+                j = g * GROUP + u
+                score_gradients(SECOND, j, delta)
+                keep(0, j, jnp.dot(expo[j], q_rows[...], preferred_element_type=F32) * SCALE)
+
+        for g in reversed(range(WINDOW // GROUP + 1)):
+            pl.when(g < groups)(functools.partial(group, g))
+            after_group(0, g)
+
+    def backward_queries(s):
+        first, heads, span, n = part(s)
+        dq_t[:, :n] = jnp.zeros((HD, n), F32)
+
+        @pl.loop(0, groups)
+        def _(g):
             keys = pl.ds(pl.multiple_of(g * GROUP * rows, rows), GROUP * rows)
-            dq_t[:, :n] += jnp.dot(
-                key_t[:, keys], jnp.concatenate(all_ds, axis=0), preferred_element_type=F32
-            )
-
-        if last:
-            for g in reversed(range(WINDOW // GROUP + 1)):
-                pl.when(g < groups)(functools.partial(group, g))
-                after_group(g)
-        else:
-            pl.loop(0, groups)(group)
+            ds = jnp.concatenate([expo[g * GROUP + u, :, span] for u in range(GROUP)], axis=0)
+            dq_t[:, :n] += jnp.dot(key_t[:, keys], ds, preferred_element_type=F32)
 
         inner = jnp.zeros((1, rows), F32)
         for i in range(heads):
-            r = off // HD + i
+            r = first + i
             one = dq_t[:, i * rows : (i + 1) * rows] * SCALE
             dproj[h, :, r * HD : (r + 1) * HD] = jnp.transpose(one).astype(BF16)
             inner += jnp.sum(one * q_t[:, r * rows : (r + 1) * rows].astype(F32), 0, keepdims=True)
@@ -484,34 +509,45 @@
             landed_piece(s, 4 + n, who, 0, rows)
             add(s, who)
 
-    delta = forward(1)
-    inner = backward(1, delta, False)
-    gather_send(1)
-    queries(2)
-    delta = forward(2)
-    inner += backward(2, delta, True)
-    gather_send(2)
-    gather_pass(1)
-    add_own(1, True)
-    pair_second()
-    add_rest(1)
-    gather_pass(2)
-    pair_third()
-
-    pair_grad = pair_acc[0]
-    dproj[h, :, PIECES[0][0] :] = pair_grad.astype(BF16)
-    gather_send(0)
-    prod = pair_grad[:, :HD] * window[0, :rows].astype(F32) + pair_grad[:, HD:] * window[0, rows:seg_at].astype(F32)
+    top = score(FIRST)
+    share_last(1)
+    prepare_values()
+    delta_first = output(FIRST, top)
+    queries(SECOND)
+    delta_second = output(SECOND, score(SECOND))
+    backward_values()
+    backward_first(delta_first)
+    inner = backward_queries(FIRST)
+    gather_send(FIRST)
+    backward_keys(delta_second)
+    inner += backward_queries(SECOND)
+    gather_send(SECOND)
+    pair_second(1)
+    gather_pass(FIRST)
+    add_own(FIRST, True)
+    pair_second(0)
+    pair_third(1)
+    dproj[h, :, PIECES[VALUES][0] :] = pair_acc[1, 0].astype(BF16)
+    gather_send(VALUES)
+    add_rest(FIRST)
+    gather_pass(SECOND)
+    pair_third(0)
+    dproj[h, :, PIECES[KEYS][0] : PIECES[VALUES][0]] = pair_acc[0, 0].astype(BF16)
+    gather_send(KEYS)
+    prod = pair_acc[0, 0] * key_win[0, :rows].astype(F32) + pair_acc[1, 0] * value_win[0].astype(F32)
     inner += jnp.sum(jnp.transpose(prod), 0, keepdims=True)
     inner_stats[0] = jnp.broadcast_to(inner, (8, rows))
     small_first(inner_stats, in_send, in_recv)
-    add_own(2)
+    add_own(SECOND)
+    add_rest(SECOND)
+    gather_pass(VALUES)
     small_second(inner_stats, in_send, in_recv)
-    gather_pass(0)
-    add_rest(2)
-    add_own(0)
+    add_own(VALUES)
+    add_rest(VALUES)
+    gather_pass(KEYS)
+    add_own(KEYS)
     inner_col = small_total(inner_stats, in_recv)
-    add_rest(0)
+    add_rest(KEYS)
 
     scale = recip[:, :1]
     weighted = tok[...].astype(F32) * scale
@@ -551,6 +587,7 @@
     rows, wide = tokens.shape
     group = qkv_weight.shape[1] // 8
     n = 3 * rows
+    every = HEADS * rows
     slots = WINDOW + 1
     vmem = pl.BlockSpec(memory_space=pltpu.VMEM)
     anywhere = pl.BlockSpec(memory_space=pl.ANY)
@@ -558,19 +595,20 @@
         ((rows, wide), BF16), ((8, wide, group), BF16),
         ((4, rows, group), BF16), ((4, rows, group), BF16), ((3, rows, group), BF16),
         ((2, rows // 2, group), F32), ((rows, group), F32),
-        ((2, rows // 2, group), BF16), ((2, rows, group), BF16), ((rows, 2 * HD), BF16),
-        ((6, 8, rows), F32), ((rows, HD), F32), ((slots, 2 * rows + 16, HD), BF16),
+        ((2, rows // 2, group), BF16), ((2, rows, group), BF16), ((2, rows, HD), BF16),
+        ((6, 8, rows), F32), ((rows, HD), F32),
+        ((slots, rows + 16, HD), BF16), ((slots, rows, HD), BF16),
         ((HD, slots * rows), BF16), ((HD, slots * rows), BF16), ((slots, rows, rows), F32),
         ((HEADS * rows, HD), BF16), ((HD, HEADS * rows), BF16), ((HD, HEADS * rows), BF16),
-        ((slots, rows, n), F32), ((slots, rows, n), BF16), ((HD, n), F32),
-        ((n, HD), BF16), ((HD, n), BF16), ((HD, n), F32),
-        ((slots, rows, 2 * HD), F32), ((slots, rows, 2 * HD), BF16), ((slots, rows, 2 * HD), BF16),
+        ((slots, rows, every), F32), ((slots, rows, every), BF16), ((HD, n), F32),
+        ((every, HD), BF16), ((HD, every), BF16), ((HD, n), F32),
+        ((2, slots, rows, HD), F32), ((2, slots, rows, HD), BF16), ((2, slots, rows, HD), BF16),
         ((8, rows, group), BF16), ((6, 8, rows), F32), ((rows, wide), F32), ((n_ctx, 8, 128), F32),
     ]
     sems = [
-        (3, 8), (3, 4), (3, 4), (3, 2), (3, 2), (3, 4), (3, 4), (4,), (4,),
-        (12,), (slots,), (slots,), (slots,),
-        (3, 7), (3, 7), (4,), (4,), (n_ctx,), (n_ctx,),
+        (4, 8), (4, 4), (4, 4), (4, 2), (4, 2), (4, 4), (4, 4), (4,), (4,),
+        (2, 12), (2, slots), (2, slots), (2, slots),
+        (4, 7), (4, 7), (4,), (4,), (n_ctx,), (n_ctx,),
     ]
     out_types = (
         jax.ShapeDtypeStruct((rows, HEADS * HD), BF16),

time: 90.5 us -> 83 us (0.917)
  Pallas kernels: 89.7 us -> 82.2 us
    pallas_call x1, Pallas kernels: 87.8 us -> 80.2 us  [on_device(): pl.pallas_call(functools.partial(kernel, n_ctx), out_shape=(*out_types, j...]
where the time goes in v3:
time: 83 us; the launch traced here: 82.8 us
  Pallas kernels  82.2 us (99%)
    pallas_call x1, Pallas kernels, on_device(): pl.pallas_call(functools.partial(kernel, n_ctx), out_shape=(*out_types, j...  80.2 us
    pallas_call x1, Pallas kernels, on_device(): pl.pallas_call(hand_over, out_shape=(*out_types, jax.ShapeDtypeStruct((wi...  1.94 us

profile of v3, /device:TPU:0, one launch (start us, length us, event | category | flops | bytes accessed | tf_op | source)
XLA Modules:
  0.0 82.8 jit_solution(11206469218027792199)
XLA Ops:
  0.6 80.2 %shard_map.85 = (bf16[256,640]{1,0:T(8,128)(2,1)}, bf16[256,640]{1,0:T(8,128)(2,1)}, f32[8,128]{1,0:T(8,128)}) custom-call(bf16[256,640]{1,0:T(8,128)(2,1)} %tok.1, f32[640]{0:T(1024)} %gain.1, bf16[640,7168]{1,0:T(8,128)(2,1)} %w_hbm.1, bf16[256,640]{1,0:T(8,128)(2,1)} %target.1, s32[1,256]{1,0:T(1,128)} %bitcast.2, s32[1,256]{1,0:T(1,128)} %bitcast.3), custom_call_target="tpu_custom_call" | custom-call | tf_op jit(solution)/shard_map/pallas_call | solution.py:617
  80.9 1.9 %shard_map.86 = (bf16[256,640]{1,0:T(8,128)(2,1)}, bf16[256,640]{1,0:T(8,128)(2,1)}, f32[640]{0:T(1024)}) custom-call(bf16[256,640]{1,0:T(8,128)(2,1)} %get-tuple-element.6.attn, bf16[256,640]{1,0:T(8,128)(2,1)} %get-tuple-element.7.grad_tokens, f32[8,128]{1,0:T(8,128)} %get-tuple-element.8.gain_rows), custom_call_target="tpu_custom_call" | custom-call | tf_op jit(solution)/shard_map/pallas_call | solution.py:631

commit v4 on v3

--- a/solution.py
+++ b/solution.py
@@ -94,7 +94,10 @@
             fetch(s, i)[1].start()
 
     gain_row = gain[...].reshape(1, wide_in)
-    xb[...] = (tok[...].astype(F32) * gain_row).astype(BF16)
+    features = tok[...].astype(F32)
+    xb[...] = (features * gain_row).astype(BF16)
+    squares = jnp.sum(features * features, -1, keepdims=True)
+    stats[0] = jnp.transpose(jnp.broadcast_to(squares, (rows, HD)))[:8]
 
     def project(s):
         off, wide = PIECES[s]
@@ -107,10 +110,13 @@
             ).astype(BF16)
             if s == 0 and i == 0:
                 pl.semaphore_wait(barrier, 4 + len(others))
+                small_first(stats, st_send, st_recv)
             start(remote(
                 part_send.at[i, :, cols], part_recv.at[i, :, cols],
                 ps_send.at[s, i], ps_recv.at[s, i], head=partner,
             ))
+        if s == KEYS:
+            small_second(stats, st_send, st_recv)
         for i in range(4):
             g, copy = fetch(s, 4 + i)
             copy.wait()
@@ -208,14 +214,7 @@
         return jnp.transpose(ref[2] + ref[3] + ref[4] + ref[5])[:, :1]
 
     project(KEYS)
-    features = tok[...].astype(F32)
-    stats[0] = lax.dot_general(
-        jnp.ones((8, wide_in), F32), features * features, (((1,), (1,)), ((), ())),
-        precision=lax.Precision.HIGHEST, preferred_element_type=F32,
-    )
-    small_first(stats, st_send, st_recv)
     project(VALUES)
-    small_second(stats, st_send, st_recv)
     seg_row = segment[...].astype(F32)
     which = lax.broadcasted_iota(jnp.int32, (16, HD), 0)
     seg_block = jnp.zeros((16, HD), F32)
@@ -313,14 +312,18 @@
         key_win[j] = jnp.zeros((rows + 16, HD), BF16)
         value_win[j] = jnp.zeros((rows, HD), BF16)
         key_t[:, span] = jnp.zeros((HD, rows), BF16)
+        value_t[:, span] = jnp.zeros((HD, rows), BF16)
         bias[j] = jnp.full((rows, rows), HIDDEN, F32)
 
     def prepare_values():
-        @pl.loop(0, groups * GROUP)
-        def _(j):
-            value_t[:, pl.ds(pl.multiple_of(j * rows, rows), rows)] = (
-                jnp.transpose(value_win[j].astype(F32)).astype(BF16)
-            )
+        for j in (0, 4, 1, 2, 3, 8, 5, 6, 7):
+            if j % 4:
+                here(1, j)
+
+            def one(j=j):
+                value_t[:, j * rows : (j + 1) * rows] = jnp.transpose(value_win[j].astype(F32)).astype(BF16)
+
+            pl.when(c >= j)(one)
 
     def part(s):
         off, wide = PIECES[s]
@@ -509,12 +512,12 @@
             landed_piece(s, 4 + n, who, 0, rows)
             add(s, who)
 
-    top = score(FIRST)
-    share_last(1)
+    top_first = score(FIRST)
+    queries(SECOND)
+    top_second = score(SECOND)
     prepare_values()
-    delta_first = output(FIRST, top)
-    queries(SECOND)
-    delta_second = output(SECOND, score(SECOND))
+    delta_first = output(FIRST, top_first)
+    delta_second = output(SECOND, top_second)
     backward_values()
     backward_first(delta_first)
     inner = backward_queries(FIRST)
@@ -530,10 +533,10 @@
     dproj[h, :, PIECES[VALUES][0] :] = pair_acc[1, 0].astype(BF16)
     gather_send(VALUES)
     add_rest(FIRST)
-    gather_pass(SECOND)
     pair_third(0)
     dproj[h, :, PIECES[KEYS][0] : PIECES[VALUES][0]] = pair_acc[0, 0].astype(BF16)
     gather_send(KEYS)
+    gather_pass(SECOND)
     prod = pair_acc[0, 0] * key_win[0, :rows].astype(F32) + pair_acc[1, 0] * value_win[0].astype(F32)
     inner += jnp.sum(jnp.transpose(prod), 0, keepdims=True)
     inner_stats[0] = jnp.broadcast_to(inner, (8, rows))

time: 83 us -> 78.3 us (0.943)
  Pallas kernels: 82.2 us -> 77.5 us
    pallas_call x1, Pallas kernels: 80.2 us -> 75.6 us  [on_device(): pl.pallas_call(functools.partial(kernel, n_ctx), out_shape=(*out_types, j...]
where the time goes in v4:
time: 78.3 us; the launch traced here: 78.2 us
  Pallas kernels  77.5 us (99%)
    pallas_call x1, Pallas kernels, on_device(): pl.pallas_call(functools.partial(kernel, n_ctx), out_shape=(*out_types, j...  75.6 us
    pallas_call x1, Pallas kernels, on_device(): pl.pallas_call(hand_over, out_shape=(*out_types, jax.ShapeDtypeStruct((wi...  1.94 us

profile of v4, /device:TPU:0, one launch (start us, length us, event | category | flops | bytes accessed | tf_op | source)
XLA Modules:
  0.0 78.2 jit_solution(1886793443155936498)
XLA Ops:
  0.6 75.6 %shard_map.85 = (bf16[256,640]{1,0:T(8,128)(2,1)}, bf16[256,640]{1,0:T(8,128)(2,1)}, f32[8,128]{1,0:T(8,128)}) custom-call(bf16[256,640]{1,0:T(8,128)(2,1)} %tok.1, f32[640]{0:T(1024)} %gain.1, bf16[640,7168]{1,0:T(8,128)(2,1)} %w_hbm.1, bf16[256,640]{1,0:T(8,128)(2,1)} %target.1, s32[1,256]{1,0:T(1,128)} %bitcast.2, s32[1,256]{1,0:T(1,128)} %bitcast.3), custom_call_target="tpu_custom_call" | custom-call | tf_op jit(solution)/shard_map/pallas_call | solution.py:620
  76.2 1.9 %shard_map.86 = (bf16[256,640]{1,0:T(8,128)(2,1)}, bf16[256,640]{1,0:T(8,128)(2,1)}, f32[640]{0:T(1024)}) custom-call(bf16[256,640]{1,0:T(8,128)(2,1)} %get-tuple-element.6.attn, bf16[256,640]{1,0:T(8,128)(2,1)} %get-tuple-element.7.grad_tokens, f32[8,128]{1,0:T(8,128)} %get-tuple-element.8.gain_rows), custom_call_target="tpu_custom_call" | custom-call | tf_op jit(solution)/shard_map/pallas_call | solution.py:634

commit v5 on v4

--- a/solution.py
+++ b/solution.py
@@ -67,8 +67,26 @@
         else:
             pl.when(when)(copy.start)
 
+    def settle(copies):
+        for copy, when in copies:
+            if when is None:
+                copy.wait_send()
+            else:
+                pl.when(when)(copy.wait_send)
+
     def arrived(dst, recv):
         remote(dst, dst, recv, recv, head=partner).wait_recv()
+
+    def fetch(s, i):
+        off, wide = PIECES[s]
+        g = head_of(x + STEPS[i % 4], (1 - p) if i < 4 else p)
+        first = pl.multiple_of(g * 896 + off, 128)
+        return g, pltpu.make_async_copy(
+            w_hbm.at[:, pl.ds(first, wide)], wv.at[g, :, pl.ds(off, wide)], w_sem.at[s, i]
+        )
+
+    for i in range(8):
+        fetch(KEYS, i)[1].start()
 
     barrier = pltpu.get_barrier_semaphore()
     for other in (partner, right, left, head_of(x + 2, p)):
@@ -81,15 +99,7 @@
             barrier, inc=1, device_id={"ctx": other}, device_id_type=pl.DeviceIdType.MESH
         )
 
-    def fetch(s, i):
-        off, wide = PIECES[s]
-        g = head_of(x + STEPS[i % 4], (1 - p) if i < 4 else p)
-        first = pl.multiple_of(g * 896 + off, 128)
-        return g, pltpu.make_async_copy(
-            w_hbm.at[:, pl.ds(first, wide)], wv.at[g, :, pl.ds(off, wide)], w_sem.at[s, i]
-        )
-
-    for s in range(4):
+    for s in range(1, 4):
         for i in range(8):
             fetch(s, i)[1].start()
 
@@ -419,10 +429,13 @@
             take(w, j, 0, z + j // 4 < rings)
 
     def backward_values():
+        later = part(SECOND)[2]
+
         def group(g):
             for u in reversed(range(GROUP)):
                 j = g * GROUP + u
-                keep(1, j, jnp.dot(expo[j], gp_rows[...], preferred_element_type=F32))
+                dv = jnp.dot(expo[j, :, later], gp_rows[later], preferred_element_type=F32)
+                keep(1, j, pair_acc[1, j] + dv)
 
         for g in reversed(range(WINDOW // GROUP + 1)):
             pl.when(g < groups)(functools.partial(group, g))
@@ -434,10 +447,14 @@
         expo[j, :, span] = (expo[j, :, span].astype(F32) * (dp - delta)).astype(BF16)
 
     def backward_first(delta):
+        sooner = part(FIRST)[2]
+
         @pl.loop(0, groups)
         def _(g):
             for u in range(GROUP):
-                score_gradients(FIRST, g * GROUP + u, delta)
+                j = g * GROUP + u
+                pair_acc[1, j] = jnp.dot(expo[j, :, sooner], gp_rows[sooner], preferred_element_type=F32)
+                score_gradients(FIRST, j, delta)
 
     def backward_keys(delta):
         def group(g):
@@ -480,7 +497,7 @@
         arrived(slot(dproj, s, who, lo, size), ag_recv.at[s, n])
 
     def gather_send(s):
-        for n, to in enumerate((right, left, far, partner)):
+        for n, to in ((3, partner), (2, far), (0, right), (1, left)):
             move(s, n, h, 0, rows, to)
 
     def gather_pass(s):
@@ -517,11 +534,11 @@
     top_second = score(SECOND)
     prepare_values()
     delta_first = output(FIRST, top_first)
-    delta_second = output(SECOND, top_second)
-    backward_values()
     backward_first(delta_first)
     inner = backward_queries(FIRST)
     gather_send(FIRST)
+    delta_second = output(SECOND, top_second)
+    backward_values()
     backward_keys(delta_second)
     inner += backward_queries(SECOND)
     gather_send(SECOND)
@@ -559,6 +576,7 @@
     gain_stats[0] = jnp.zeros((8, 128), F32)
     for k in range(lanes):
         gain_stats[0, k : k + 1] = gain_part[:, k * 128 : (k + 1) * 128]
+    before = len(started)
     for d in range(1, n_ctx):
         start(remote(
             gain_stats.at[0], gain_stats.at[d], gg_send.at[d], gg_recv.at[d], ctx=lax.rem(c + d, n_ctx),
@@ -566,17 +584,14 @@
     grad_tokens[...] = (
         dnormed[...] * gain[...].reshape(1, wide_in) * scale - weighted * (scale * inner_col * (1.0 / D))
     ).astype(BF16)
+    settle(started[:before])
     gain_total = gain_stats[0]
     for d in range(1, n_ctx):
         arrived(gain_stats.at[d], gg_recv.at[d])
         gain_total = gain_total + gain_stats[d]
     grad_gain[...] = gain_total
 
-    for copy, when in started:
-        if when is None:
-            copy.wait_send()
-        else:
-            pl.when(when)(copy.wait_send)
+    settle(started[before:])
 
 
 def hand_over(attn, grad_tokens, gain_rows, attn_out, grad_out, gain_out):

time: 78.3 us -> 77 us (0.983)
  Pallas kernels: 77.5 us -> 76.2 us
    pallas_call x1, Pallas kernels: 75.6 us -> 74.2 us  [on_device(): pl.pallas_call(functools.partial(kernel, n_ctx), out_shape=(*out_types, j...]
where the time goes in v5:
time: 77 us; the launch traced here: 76.8 us
  Pallas kernels  76.2 us (99%)
    pallas_call x1, Pallas kernels, on_device(): pl.pallas_call(functools.partial(kernel, n_ctx), out_shape=(*out_types, j...  74.2 us
    pallas_call x1, Pallas kernels, on_device(): pl.pallas_call(hand_over, out_shape=(*out_types, jax.ShapeDtypeStruct((wi...  1.94 us

profile of v5, /device:TPU:0, one launch (start us, length us, event | category | flops | bytes accessed | tf_op | source)
XLA Modules:
  0.0 76.8 jit_solution(9637020339898145238)
XLA Ops:
  0.6 74.2 %shard_map.85 = (bf16[256,640]{1,0:T(8,128)(2,1)}, bf16[256,640]{1,0:T(8,128)(2,1)}, f32[8,128]{1,0:T(8,128)}) custom-call(bf16[256,640]{1,0:T(8,128)(2,1)} %tok.1, f32[640]{0:T(1024)} %gain.1, bf16[640,7168]{1,0:T(8,128)(2,1)} %w_hbm.1, bf16[256,640]{1,0:T(8,128)(2,1)} %target.1, s32[1,256]{1,0:T(1,128)} %bitcast.2, s32[1,256]{1,0:T(1,128)} %bitcast.3), custom_call_target="tpu_custom_call" | custom-call | tf_op jit(solution)/shard_map/pallas_call | solution.py:635
  74.9 1.9 %shard_map.86 = (bf16[256,640]{1,0:T(8,128)(2,1)}, bf16[256,640]{1,0:T(8,128)(2,1)}, f32[640]{0:T(1024)}) custom-call(bf16[256,640]{1,0:T(8,128)(2,1)} %get-tuple-element.6.attn, bf16[256,640]{1,0:T(8,128)(2,1)} %get-tuple-element.7.grad_tokens, f32[8,128]{1,0:T(8,128)} %get-tuple-element.8.gain_rows), custom_call_target="tpu_custom_call" | custom-call | tf_op jit(solution)/shard_map/pallas_call | solution.py:649

commit v6 on v5

--- a/solution.py
+++ b/solution.py
@@ -498,7 +498,21 @@
 
     def gather_send(s):
         for n, to in ((3, partner), (2, far), (0, right), (1, left)):
-            move(s, n, h, 0, rows, to)
+            if s != SECOND or n != 2:
+                move(s, n, h, 0, rows, to)
+
+    def gather_on(s):
+        landed_piece(s, 0, left, 0, rows)
+        move(s, 2, left, 0, half, right)
+        landed_piece(s, 1, right, 0, rows)
+        move(s, 7, right, half, half, left)
+        move(s, 4, left, 0, rows, partner)
+        move(s, 5, right, 0, rows, partner)
+
+    def gather_far(s):
+        landed_piece(s, 2, far, 0, half)
+        landed_piece(s, 7, far, half, half)
+        move(s, 6, far, 0, rows, partner)
 
     def gather_pass(s):
         for n, who in enumerate((left, right, far)):
@@ -546,6 +560,7 @@
     gather_pass(FIRST)
     add_own(FIRST, True)
     pair_second(0)
+    gather_on(SECOND)
     pair_third(1)
     dproj[h, :, PIECES[VALUES][0] :] = pair_acc[1, 0].astype(BF16)
     gather_send(VALUES)
@@ -553,7 +568,7 @@
     pair_third(0)
     dproj[h, :, PIECES[KEYS][0] : PIECES[VALUES][0]] = pair_acc[0, 0].astype(BF16)
     gather_send(KEYS)
-    gather_pass(SECOND)
+    gather_far(SECOND)
     prod = pair_acc[0, 0] * key_win[0, :rows].astype(F32) + pair_acc[1, 0] * value_win[0].astype(F32)
     inner += jnp.sum(jnp.transpose(prod), 0, keepdims=True)
     inner_stats[0] = jnp.broadcast_to(inner, (8, rows))
@@ -626,7 +641,7 @@
     sems = [
         (4, 8), (4, 4), (4, 4), (4, 2), (4, 2), (4, 4), (4, 4), (4,), (4,),
         (2, 12), (2, slots), (2, slots), (2, slots),
-        (4, 7), (4, 7), (4,), (4,), (n_ctx,), (n_ctx,),
+        (4, 8), (4, 8), (4,), (4,), (n_ctx,), (n_ctx,),
     ]
     out_types = (
         jax.ShapeDtypeStruct((rows, HEADS * HD), BF16),

time: 77 us -> 80.2 us (1.042)
  Pallas kernels: 76.2 us -> 79.1 us
    pallas_call x1, Pallas kernels: 74.2 us -> 77.2 us  [on_device(): pl.pallas_call(functools.partial(kernel, n_ctx), out_shape=(*out_types, j...]
where the time goes in v6:
time: 80.2 us; the launch traced here: 79.8 us
  Pallas kernels  79.1 us (99%)
    pallas_call x1, Pallas kernels, on_device(): pl.pallas_call(functools.partial(kernel, n_ctx), out_shape=(*out_types, j...  77.2 us
    pallas_call x1, Pallas kernels, on_device(): pl.pallas_call(hand_over, out_shape=(*out_types, jax.ShapeDtypeStruct((wi...  1.94 us

profile of v6, /device:TPU:0, one launch (start us, length us, event | category | flops | bytes accessed | tf_op | source)
XLA Modules:
  0.0 79.8 jit_solution(7363114749542277964)
XLA Ops:
  0.6 77.2 %shard_map.85 = (bf16[256,640]{1,0:T(8,128)(2,1)}, bf16[256,640]{1,0:T(8,128)(2,1)}, f32[8,128]{1,0:T(8,128)}) custom-call(bf16[256,640]{1,0:T(8,128)(2,1)} %tok.1, f32[640]{0:T(1024)} %gain.1, bf16[640,7168]{1,0:T(8,128)(2,1)} %w_hbm.1, bf16[256,640]{1,0:T(8,128)(2,1)} %target.1, s32[1,256]{1,0:T(1,128)} %bitcast.2, s32[1,256]{1,0:T(1,128)} %bitcast.3), custom_call_target="tpu_custom_call" | custom-call | tf_op jit(solution)/shard_map/pallas_call | solution.py:650
  77.9 1.9 %shard_map.86 = (bf16[256,640]{1,0:T(8,128)(2,1)}, bf16[256,640]{1,0:T(8,128)(2,1)}, f32[640]{0:T(1024)}) custom-call(bf16[256,640]{1,0:T(8,128)(2,1)} %get-tuple-element.6.attn, bf16[256,640]{1,0:T(8,128)(2,1)} %get-tuple-element.7.grad_tokens, f32[8,128]{1,0:T(8,128)} %get-tuple-element.8.gain_rows), custom_call_target="tpu_custom_call" | custom-call | tf_op jit(solution)/shard_map/pallas_call | solution.py:664
